TPU v7x, 32 devices: a whole 2x2x4 slice. The times are simulated.
32 devices in a mesh: grp: 8 (over y, x, core), mem: 4 (over z).
Axes of the slice: x: 2, y: 2, z: 4, core: 2. Of those that a mesh axis runs over, the one named last changes fastest.
Arguments:
- filterbank: float32 [8, 4, 8, 16000], P('grp', 'mem'), may hold values from -6 to 6
- destination: int32 [8, 32], P('grp', 'mem'), may hold values from 0 to 7, as said below
- initial_conv_weight: bfloat16 [400, 1024], replicated, may hold values from -0.3125 to 0.3125
- expand_weight: bfloat16 [1024, 1024], replicated, may hold values from -0.1875 to 0.1875
- branch_weight: bfloat16 [7, 384, 128], replicated, may hold values from -0.3125 to 0.3125
- merge_weight: bfloat16 [1024, 1024], replicated, may hold values from -0.1875 to 0.1875
- squeeze_weight: bfloat16 [1024, 128], replicated, may hold values from -0.1875 to 0.1875
- excite_weight: bfloat16 [128, 1024], replicated, may hold values from -0.5 to 0.5
- attend_weight: bfloat16 [8, 3072, 128], P('grp'), may hold values from -0.1875 to 0.1875
- score_weight: bfloat16 [8, 128, 1024], P('grp'), may hold values from -0.5 to 0.5
- embed_weight: bfloat16 [8, 2048, 192], P('grp'), may hold values from -0.125 to 0.125
- language_weight: bfloat16 [8, 192, 107], P('grp'), may hold values from -0.4375 to 0.4375
Outputs:
- language_logits: float32 [8, 32, 107], P('grp', 'mem')
- similarity: float32 [8, 32, 32], P('grp', 'mem')
Inputs may be any that keep to these rules, and one draw needn't show every extreme that they name: `destination`: each device sends its 8 segments to 8 different groups, so at most 1 to any group. For every index of mem, one group receives exactly 8 segments from the devices of that index, and no group receives more.
All inputs are finite; a program needn't handle non-finite values.
Results may differ from a plain program's by a relative error of at most 0.0075.
Values may be sent and summed in bfloat16 or wider, within the bound.
A program may use at most 128 MiB of HBM per device.

v0:
```python
import jax
import jax.numpy as jnp
from jax import lax
from jax.sharding import PartitionSpec as P

MELS = 80
SCALE = 8
BRANCH_DILATION = 2
FRAMES = 200
CAP = 1


EPS_STAT = 1e-05
EPS_NORM = 1e-06


def offset_frames(values, radius, spacing):
    frames = values.shape[1]
    padded = jnp.pad(values, ((0, 0), (radius * spacing, radius * spacing), (0, 0)))
    return jnp.concatenate(
        [
            padded[:, offset * spacing : offset * spacing + frames]
            for offset in range(2 * radius + 1)
        ],
        axis=2,
    )


def trunk(
    features,
    initial_conv_weight,
    expand_weight,
    branch_weight,
    merge_weight,
    squeeze_weight,
    excite_weight,
):
    columns = offset_frames(features, 2, 1)
    front_out = jax.nn.relu(
        jnp.einsum("nfk,kc->nfc", columns, initial_conv_weight, preferred_element_type=jnp.float32)
    ).astype(jnp.bfloat16)
    expanded = jax.nn.relu(
        jnp.einsum("nfk,kc->nfc", front_out, expand_weight, preferred_element_type=jnp.float32)
    ).astype(jnp.bfloat16)
    branch_width = expanded.shape[2] // SCALE
    pieces = [expanded[:, :, :branch_width]]
    previous = expanded[:, :, :branch_width]
    for branch in range(1, SCALE):
        present_frames = expanded[:, :, branch * branch_width : (branch + 1) * branch_width]
        if branch > 1:
            present_frames = (
                present_frames.astype(jnp.float32) + previous.astype(jnp.float32)
            ).astype(jnp.bfloat16)
        stacked_rows = offset_frames(present_frames, 1, BRANCH_DILATION)
        previous = jax.nn.relu(
            jnp.einsum(
                "nfk,kc->nfc",
                stacked_rows,
                branch_weight[branch - 1],
                preferred_element_type=jnp.float32,
            )
        ).astype(jnp.bfloat16)
        pieces.append(previous)
    joined = jnp.concatenate(pieces, axis=2)
    merged = jax.nn.relu(
        jnp.einsum("nfk,kc->nfc", joined, merge_weight, preferred_element_type=jnp.float32)
    )
    squeezed = jnp.mean(merged, axis=1)
    hidden = jax.nn.relu(
        jnp.dot(squeezed, squeeze_weight.astype(jnp.float32), precision=lax.Precision.HIGHEST)
    )
    excited = jax.nn.sigmoid(
        jnp.dot(hidden, excite_weight.astype(jnp.float32), precision=lax.Precision.HIGHEST)
    )
    return (front_out.astype(jnp.float32) + merged * excited[:, None, :]).astype(jnp.bfloat16)


def head(trunk_out, attend_weight, score_weight, embed_weight, language_weight):
    channels = trunk_out.shape[1]
    widened = trunk_out.astype(jnp.float32)
    center = jnp.mean(widened, axis=0)
    spread = jnp.sqrt(jnp.mean(jnp.square(widened - center), axis=0) + EPS_STAT)
    context = jnp.dot(
        center,
        attend_weight[channels : 2 * channels].astype(jnp.float32),
        precision=lax.Precision.HIGHEST,
    )
    context = context + jnp.dot(
        spread, attend_weight[2 * channels :].astype(jnp.float32), precision=lax.Precision.HIGHEST
    )
    attended = jnp.tanh(
        jnp.dot(trunk_out, attend_weight[:channels], preferred_element_type=jnp.float32) + context
    ).astype(jnp.bfloat16)
    signal_energy = jnp.dot(attended, score_weight, preferred_element_type=jnp.float32)
    weights = jnp.exp(signal_energy)
    weights = weights / jnp.sum(weights, axis=0)
    pooled_mean = jnp.sum(weights * widened, axis=0)
    pooled_std = jnp.sqrt(jnp.sum(weights * jnp.square(widened - pooled_mean), axis=0) + EPS_STAT)
    pooled_features = jnp.concatenate([pooled_mean, pooled_std]).astype(jnp.bfloat16)
    embedding = jnp.dot(pooled_features, embed_weight, preferred_element_type=jnp.float32)
    logits = jnp.dot(
        embedding.astype(jnp.bfloat16), language_weight, preferred_element_type=jnp.float32
    )
    return (embedding, logits)


def compact(flags, most_rows):
    occupied = flags.reshape(-1)
    position_index = jnp.cumsum(occupied) - 1.0
    targets = jnp.arange(most_rows, dtype=jnp.float32)[:, None]
    return ((targets == position_index[None, :]) & (occupied[None, :] > 0.5)).astype(jnp.float32)


def shards(
    filterbank,
    destination,
    initial_conv_weight,
    expand_weight,
    branch_weight,
    merge_weight,
    squeeze_weight,
    excite_weight,
    attend_weight,
    score_weight,
    embed_weight,
    language_weight,
):
    groups = lax.axis_size("grp")
    stored = filterbank.shape[2]
    most_rows = min(2 * stored, groups)
    flat_bank = filterbank.reshape(stored, FRAMES * MELS)
    targets = destination.reshape(stored)
    positions = jnp.arange(stored, dtype=jnp.int32)
    earlier = (targets[None, :] == targets[:, None]) & (positions[None, :] < positions[:, None])
    ranking = jnp.sum(earlier, axis=1)
    outgoing = (
        jnp.arange(groups * CAP, dtype=jnp.int32)[:, None] == (targets * CAP + ranking)[None, :]
    ).astype(jnp.float32)
    send_flags = jnp.sum(outgoing, axis=1).reshape(groups, CAP)
    group_head = jax.vmap(head, in_axes=(0, None, None, None, None))
    lowered_bank = flat_bank.astype(jnp.bfloat16)
    outbound = jnp.dot(
        outgoing.astype(jnp.bfloat16), lowered_bank, preferred_element_type=jnp.float32
    )
    outbound = outbound.astype(jnp.bfloat16).reshape(groups, CAP, FRAMES * MELS)
    arrived, arrived_flags = (
        lax.all_to_all(outbound, "grp", split_axis=0, concat_axis=0, tiled=True),
        lax.all_to_all(
            send_flags.astype(jnp.bfloat16), "grp", split_axis=0, concat_axis=0, tiled=True
        ),
    )
    picker = compact(arrived_flags.astype(jnp.float32), most_rows)
    packed = jnp.dot(
        picker.astype(jnp.bfloat16),
        arrived.reshape(groups * CAP, FRAMES * MELS),
        preferred_element_type=jnp.float32,
    )
    packed = packed.astype(jnp.bfloat16)
    trunk_rows = trunk(
        packed.reshape(most_rows, FRAMES, MELS),
        initial_conv_weight,
        expand_weight,
        branch_weight,
        merge_weight,
        squeeze_weight,
        excite_weight,
    )
    embedding, logits = group_head(
        trunk_rows, attend_weight[0], score_weight[0], embed_weight[0], language_weight[0]
    )
    back_embed = jnp.dot(picker.T, embedding, precision=lax.Precision.HIGHEST).reshape(
        groups, CAP, -1
    )
    back_logits = jnp.dot(picker.T, logits, precision=lax.Precision.HIGHEST).reshape(
        groups, CAP, -1
    )
    home_embed, home_logits = (
        lax.all_to_all(back_embed, "grp", split_axis=0, concat_axis=0, tiled=True),
        lax.all_to_all(back_logits, "grp", split_axis=0, concat_axis=0, tiled=True),
    )
    own_embed = jnp.dot(
        outgoing.T, home_embed.reshape(groups * CAP, -1), precision=lax.Precision.HIGHEST
    )
    own_logits = jnp.dot(
        outgoing.T, home_logits.reshape(groups * CAP, -1), precision=lax.Precision.HIGHEST
    )
    normed = (
        own_embed * lax.rsqrt(jnp.mean(jnp.square(own_embed), axis=1, keepdims=True) + EPS_NORM)
    ).astype(jnp.bfloat16)
    embed_width = normed.shape[1]
    similarity = (
        lax.dot_general(
            normed,
            lax.all_gather(normed, "mem", axis=0, tiled=True),
            (((1,), (1,)), ((), ())),
            preferred_element_type=jnp.float32,
        )
        / embed_width
    )
    return (own_logits.reshape(1, stored, -1), similarity.reshape(1, stored, -1))


def solution(mesh):
    return jax.shard_map(
        shards,
        mesh=mesh,
        in_specs=(
            P("grp", "mem", None, None),
            P("grp", "mem"),
            P(),
            P(),
            P(),
            P(),
            P(),
            P(),
            P("grp", None, None),
            P("grp", None, None),
            P("grp", None, None),
            P("grp", None, None),
        ),
        out_specs=(P("grp", "mem", None), P("grp", "mem", None)),
        check_vma=False,
    )
```

profile of v0, /device:TPU:0, one launch (start us, length us, event | category | flops | bytes accessed | tf_op | source)
XLA Modules:
  0.0 113.9 jit_solution(2227953342200570258)
XLA Ops:
  3.1 5.2 %all-to-all-start = ((bf16[8,1,1]{2,1,0:T(2,128)(2,1)}), bf16[8,1,1]{2,1,0:T(2,128)(2,1)S(1)}, u32[]{:S(2)}, u32[]{:S(2)}) async-start(bf16[8,1,1]{2,1,0:T(2,128)(2,1)} %copy.22), calls=%async_computation | async-start | bytes 8192 | tf_op jit(solution)/shard_map/all_to_all | solution.py:148
  8.3 1.2 %fusion.1 = bf16[8,1,16000]{2,0,1:T(8,128)(2,1)S(1)} fusion(f32[1,1,8,16000]{3,2,1,0:T(8,128)} %param.12, s32[8]{0:T(128)S(1)} %fusion.126), kind=kOutput, calls=%fused_computation.3 | convolution fusion | flops 2304192 | bytes 768032 | tf_op jit(solution)/shard_map/dot_general | solution.py:142
  12.9 3.4 %all-to-all-start.1 = ((bf16[8,2,8000]{2,1,0:T(2,128)(2,1)}), bf16[8,2,8000]{2,1,0:T(2,128)(2,1)S(1)}, u32[]{:S(2)}, u32[]{:S(2)}) async-start(bf16[8,2,8000]{2,1,0:T(2,128)(2,1)} %reshape.143), calls=%async_computation.1 | async-start | bytes 516096 | tf_op jit(solution)/shard_map/all_to_all | solution.py:147
  16.9 6.2 %all-to-all-done.1 = bf16[8,2,8000]{2,1,0:T(2,128)(2,1)S(1)} async-done(((bf16[8,2,8000]{2,1,0:T(2,128)(2,1)}), bf16[8,2,8000]{2,1,0:T(2,128)(2,1)S(1)}, u32[]{:S(2)}, u32[]{:S(2)}) %all-to-all-start.1) | async-done | bytes 256032 | tf_op jit(solution)/shard_map/all_to_all | solution.py:147
  24.2 1.3 %pad_slice_fusion.14 = (bf16[8,200,80]{2,1,0:T(8,128)(2,1)S(1)}, bf16[8,200,80]{2,1,0:T(8,128)(2,1)S(1)}, bf16[8,200,80]{2,1,0:T(8,128)(2,1)}, bf16[8,200,80]{2,1,0:T(8,128)(2,1)}) fusion(bf16[8,200,80]{2,1,0:T(8,128)(2,1)S(1)} %reshape.121), kind=kLoop, calls=%fused_computation.113 | loop fusion | bytes 1280000 | tf_op jit(solution)/shard_map/slice | solution.py:22
  25.5 3.9 %concatenate.31 = bf16[8,200,400]{2,1,0:T(8,128)(2,1)} concatenate(bf16[8,200,80]{2,1,0:T(8,128)(2,1)} %get-tuple-element.23, bf16[8,200,80]{2,1,0:T(8,128)(2,1)S(1)} %get-tuple-element.21, bf16[8,200,80]{2,1,0:T(8,128)(2,1)S(1)} %reshape.121, bf16[8,200,80]{2,1,0:T(8,128)(2,1)} %get-tuple-element.22, bf16[8,200,80]{2,1,0:T(8,128)(2,1)S(1)} %get-tuple-element.20), dimensions={2} | concatenate | bytes 2560000 | tf_op jit(solution)/shard_map/concatenate | solution.py:20
  29.4 3.7 %maximum_convert_fusion.1 = bf16[8,200,1024]{2,1,0:T(8,128)(2,1)S(1)} fusion(bf16[8,200,400]{2,1,0:T(8,128)(2,1)} %concatenate.31, bf16[400,1024]{1,0:T(8,128)(2,1)} %param.14), kind=kOutput, calls=%fused_computation.16 | convolution fusion | flops 1313996800 | bytes 5376000 | tf_op jit(solution)/shard_map/nfk,kc->nfc/dot_general | solution.py:40
  33.1 4.0 %maximum_convert_fusion = bf16[8,200,1024]{2,1,0:T(8,128)(2,1)S(1)} fusion(bf16[8,200,1024]{2,1,0:T(8,128)(2,1)S(1)} %maximum_convert_fusion.1, bf16[1024,1024]{1,0:T(8,128)(2,1)S(1)} %copy-done.10), kind=kOutput, calls=%fused_computation.15 | convolution fusion | flops 3358720000 | bytes 8650752 | tf_op jit(solution)/shard_map/nfk,kc->nfc/dot_general | solution.py:43
  37.4 1.8 %constant_dynamic-update-slice_fusion.5 = (bf16[8,200,1024]{2,1,0:T(8,128)(2,1)S(1)}, bf16[8,200,128]{2,1,0:T(8,128)(2,1)S(1)}) fusion(bf16[8,200,1024]{2,1,0:T(8,128)(2,1)S(1)} %get-tuple-element.5, bf16[7,384,128]{2,1,0:T(8,128)(2,1)} %param.16, bf16[8,200,128]{2,1,0:T(8,128)(2,1)S(1)} %get-tuple-element.19, ...), kind=kOutput, calls=%fused_computation.158 | convolution fusion | flops 161382400 | bytes 2146304 | tf_op jit(solution)/shard_map/nfk,kc->nfc/dot_general | solution.py:56
  39.2 1.1 add_convert_fusion.6
  40.6 1.7 %constant_dynamic-update-slice_fusion.4 = (bf16[8,200,1024]{2,1,0:T(8,128)(2,1)S(1)}, bf16[8,200,128]{2,1,0:T(8,128)(2,1)S(1)}) fusion(bf16[8,200,1024]{2,1,0:T(8,128)(2,1)S(1)} %get-tuple-element.24, bf16[7,384,128]{2,1,0:T(8,128)(2,1)} %param.16, bf16[8,200,128]{2,1,0:T(8,128)(2,1)S(1)} %get-tuple-element.17, ...), kind=kOutput, calls=%fused_computation.157 | convolution fusion | flops 161382400 | bytes 2146304 | tf_op jit(solution)/shard_map/nfk,kc->nfc/dot_general | solution.py:56
  42.2 1.1 add_convert_fusion.5
  43.6 1.7 %constant_dynamic-update-slice_fusion.3 = (bf16[8,200,1024]{2,1,0:T(8,128)(2,1)S(1)}, bf16[8,200,128]{2,1,0:T(8,128)(2,1)S(1)}) fusion(bf16[8,200,1024]{2,1,0:T(8,128)(2,1)S(1)} %get-tuple-element.26, bf16[7,384,128]{2,1,0:T(8,128)(2,1)} %param.16, bf16[8,200,128]{2,1,0:T(8,128)(2,1)S(1)} %get-tuple-element.15, ...), kind=kOutput, calls=%fused_computation.156 | convolution fusion | flops 161382400 | bytes 2146304 | tf_op jit(solution)/shard_map/nfk,kc->nfc/dot_general | solution.py:56
  45.2 1.1 add_convert_fusion.4
  46.6 1.7 %constant_dynamic-update-slice_fusion.2 = (bf16[8,200,1024]{2,1,0:T(8,128)(2,1)S(1)}, bf16[8,200,128]{2,1,0:T(8,128)(2,1)S(1)}) fusion(bf16[8,200,1024]{2,1,0:T(8,128)(2,1)S(1)} %get-tuple-element.28, bf16[7,384,128]{2,1,0:T(8,128)(2,1)} %param.16, bf16[8,200,128]{2,1,0:T(8,128)(2,1)S(1)} %get-tuple-element.13, ...), kind=kOutput, calls=%fused_computation.155 | convolution fusion | flops 161382400 | bytes 2146304 | tf_op jit(solution)/shard_map/nfk,kc->nfc/dot_general | solution.py:56
  48.2 1.1 add_convert_fusion.3
  49.5 1.7 %constant_dynamic-update-slice_fusion.1 = (bf16[8,200,1024]{2,1,0:T(8,128)(2,1)S(1)}, bf16[8,200,128]{2,1,0:T(8,128)(2,1)S(1)}) fusion(bf16[8,200,1024]{2,1,0:T(8,128)(2,1)S(1)} %get-tuple-element.30, bf16[7,384,128]{2,1,0:T(8,128)(2,1)} %param.16, bf16[8,200,128]{2,1,0:T(8,128)(2,1)S(1)} %get-tuple-element.11, ...), kind=kOutput, calls=%fused_computation.154 | convolution fusion | flops 161382400 | bytes 2146304 | tf_op jit(solution)/shard_map/nfk,kc->nfc/dot_general | solution.py:56
  51.2 1.1 add_convert_fusion.2
  52.5 1.7 %constant_dynamic-update-slice_fusion = (bf16[8,200,1024]{2,1,0:T(8,128)(2,1)S(1)}, bf16[8,200,128]{2,1,0:T(8,128)(2,1)S(1)}) fusion(bf16[8,200,1024]{2,1,0:T(8,128)(2,1)S(1)} %get-tuple-element.32, bf16[7,384,128]{2,1,0:T(8,128)(2,1)} %param.16, bf16[8,200,128]{2,1,0:T(8,128)(2,1)S(1)} %get-tuple-element.9, ...), kind=kOutput, calls=%fused_computation.153 | convolution fusion | flops 161382400 | bytes 2146304 | tf_op jit(solution)/shard_map/nfk,kc->nfc/dot_general | solution.py:56
  54.2 1.1 add_convert_fusion.1
  55.5 1.6 %fusion.22 = bf16[8,200,1024]{2,1,0:T(8,128)(2,1)S(1)} fusion(bf16[8,200,1024]{2,1,0:T(8,128)(2,1)S(1)} %get-tuple-element.34, bf16[8,200,128]{2,1,0:T(8,128)(2,1)S(1)} %get-tuple-element.7, bf16[8,200,128]{2,1,0:T(8,128)(2,1)S(1)} %add_convert_fusion.1, bf16[8,200,128]{2,1,0:T(8,128)(2,1)S(1)} %get-tuple-element.6, bf16[7,384,128]{2,1,0:T(8,128)(2,1)} %param.16), kind=kOutput, calls=%fused_computation.40 | convolution fusion | flops 161382400 | bytes 1736704 | tf_op jit(solution)/shard_map/nfk,kc->nfc/dot_general | solution.py:56
  57.2 3.7 %maximum_reduce_fusion = (f32[8,1024]{1,0:T(8,128)S(1)}, f32[8,200,1024]{2,1,0:T(8,128)S(1)}) fusion(bf16[8,200,1024]{2,1,0:T(8,128)(2,1)S(1)} %fusion.22, bf16[1024,1024]{1,0:T(8,128)(2,1)S(1)} %copy-done), kind=kOutput, calls=%fused_computation.20 | convolution fusion | flops 3358711808 | bytes 11960320 | tf_op jit(solution)/shard_map/nfk,kc->nfc/dot_general | solution.py:66
  61.4 1.5 %convert_reduce_fusion = (f32[8,1024]{1,0:T(8,128)S(1)}, bf16[8,200,1024]{2,1,0:T(8,128)(2,1)S(1)}) fusion(f32[8,1024]{1,0:T(8,128)S(1)} %fusion.62, f32[8,200,1024]{2,1,0:T(8,128)S(1)} %get-tuple-element.37, bf16[8,200,1024]{2,1,0:T(8,128)(2,1)S(1)} %maximum_convert_fusion.1), kind=kLoop, calls=%fused_computation.7 | loop fusion | flops 11460608 | bytes 13172736 | tf_op jit(solution)/shard_map/vmap()/reduce_sum | solution.py:81
  63.2 1.5 %copy-done.1 = bf16[8,200,1024]{2,1,0:T(8,128)(2,1)} copy-done((bf16[8,200,1024]{2,1,0:T(8,128)(2,1)}, bf16[8,200,1024]{2,1,0:T(8,128)(2,1)S(1)}, u32[]{:S(2)}) %copy-start.1) | copy-done | bytes 3276824
  66.0 6.5 %fusion.59 = f32[8,200,1024]{2,1,0:T(8,128)} fusion(bf16[8,200,1024]{2,1,0:T(8,128)(2,1)} %copy-done.1, f32[8,128]{1,0:T(8,128)S(1)} %convolution_add_fusion.1, bf16[1,128,1024]{2,1,0:T(8,128)(2,1)S(1)} %copy-done.6, bf16[1,3072,128]{2,1,0:T(8,128)(2,1)S(1)} %copy-done.4), kind=kOutput, calls=%fused_computation.77 | convolution fusion | flops 839270400 | bytes 10358784 | tf_op jit(solution)/shard_map/vmap()/dot_general | solution.py:94
  72.5 8.5 %fusion.4 = (f32[8,1024]{1,0:T(8,128)S(1)}, f32[8,200,1024]{2,1,0:T(8,128)S(1)}) fusion(bf16[8,200,1024]{2,1,0:T(8,128)(2,1)} %copy-done.1, f32[8,200,1024]{2,1,0:T(8,128)} %fusion.59), kind=kOutput, calls=%fused_computation.10 | output fusion | flops 6553799 | bytes 16416768 | tf_op jit(solution)/shard_map/vmap()/div | solution.py:96
  81.1 1.3 %fusion.7 = f32[8,1024]{1,0:T(8,128)S(1)} fusion(f32[8,200,1024]{2,1,0:T(8,128)S(1)} %get-tuple-element.39, bf16[8,200,1024]{2,1,0:T(8,128)(2,1)S(1)} %copy-done.2, f32[8,1024]{1,0:T(8,128)S(1)} %get-tuple-element.38), kind=kLoop, calls=%fused_computation.13 | loop fusion | flops 8183808 | bytes 9895936 | tf_op jit(solution)/shard_map/vmap()/reduce_sum | solution.py:98
  83.6 3.3 %all-to-all-start.2 = ((f32[8,1,107]{2,1,0:T(1,128)}), f32[8,1,107]{2,1,0:T(1,128)S(1)}, u32[]{:S(2)}, u32[]{:S(2)}) async-start(f32[8,1,107]{2,1,0:T(1,128)} %bitcast.33), calls=%async_computation.2 | async-start | bytes 8192 | tf_op jit(solution)/shard_map/all_to_all | solution.py:179
  87.8 3.7 %all-to-all-done.2 = f32[8,1,107]{2,1,0:T(1,128)S(1)} async-done(((f32[8,1,107]{2,1,0:T(1,128)}), f32[8,1,107]{2,1,0:T(1,128)S(1)}, u32[]{:S(2)}, u32[]{:S(2)}) %all-to-all-start.2) | async-done | bytes 3456 | tf_op jit(solution)/shard_map/all_to_all | solution.py:179
  91.5 3.3 %all-to-all-start.3 = ((f32[8,1,192]{2,1,0:T(1,128)}), f32[8,1,192]{2,1,0:T(1,128)S(1)}, u32[]{:S(2)}, u32[]{:S(2)}) async-start(f32[8,1,192]{2,1,0:T(1,128)} %copy.25), calls=%async_computation.3 | async-start | bytes 16384 | tf_op jit(solution)/shard_map/all_to_all | solution.py:178
  95.6 3.9 %all-to-all-done.3 = f32[8,1,192]{2,1,0:T(1,128)S(1)} async-done(((f32[8,1,192]{2,1,0:T(1,128)}), f32[8,1,192]{2,1,0:T(1,128)S(1)}, u32[]{:S(2)}, u32[]{:S(2)}) %all-to-all-start.3) | async-done | bytes 6176 | tf_op jit(solution)/shard_map/all_to_all | solution.py:178
  99.8 13.4 %all_gather.3 = bf16[32,192]{1,0:T(8,128)(2,1)S(1)} all-gather(bf16[8,192]{1,0:T(8,128)(2,1)S(1)} %multiply_convert_fusion), channel_id=1, replica_groups=mesh['grp'=8,'mem'=4] {'mem'}, dimensions={0}, use_global_device_ids=true | all-gather | bytes 15360 | tf_op jit(solution)/shard_map/all_gather | solution.py:194
  (62 shorter events, 14.9 us)
Async XLA Ops:
  0.6 56.5 %copy-start = (bf16[1024,1024]{1,0:T(8,128)(2,1)S(1)}, bf16[1024,1024]{1,0:T(8,128)(2,1)}, u32[]{:S(2)}) copy-start(bf16[1024,1024]{1,0:T(8,128)(2,1)} %param.17) | copy-start | bytes 6291460
  3.1 9.8 %all-to-all-start = ((bf16[8,1,1]{2,1,0:T(2,128)(2,1)}), bf16[8,1,1]{2,1,0:T(2,128)(2,1)S(1)}, u32[]{:S(2)}, u32[]{:S(2)}) async-start(bf16[8,1,1]{2,1,0:T(2,128)(2,1)} %copy.22), calls=%async_computation | async-start | bytes 8192 | tf_op jit(solution)/shard_map/all_to_all | solution.py:148
  12.9 10.2 %all-to-all-start.1 = ((bf16[8,2,8000]{2,1,0:T(2,128)(2,1)}), bf16[8,2,8000]{2,1,0:T(2,128)(2,1)S(1)}, u32[]{:S(2)}, u32[]{:S(2)}) async-start(bf16[8,2,8000]{2,1,0:T(2,128)(2,1)} %reshape.143), calls=%async_computation.1 | async-start | bytes 516096 | tf_op jit(solution)/shard_map/all_to_all | solution.py:147
  29.4 3.7 %copy-start.10 = (bf16[1024,1024]{1,0:T(8,128)(2,1)S(1)}, bf16[1024,1024]{1,0:T(8,128)(2,1)}, u32[]{:S(2)}) copy-start(bf16[1024,1024]{1,0:T(8,128)(2,1)} %param.15) | copy-start | bytes 6291460
  37.1 2.2 %copy-start.3 = (bf16[8,200,1024]{2,1,0:T(8,128)(2,1)}, bf16[8,200,1024]{2,1,0:T(8,128)(2,1)S(1)}, u32[]{:S(2)}) copy-start(bf16[8,200,1024]{2,1,0:T(8,128)(2,1)S(1)} %maximum_convert_fusion) | copy-start | bytes 9830404
  57.2 3.7 %copy-start.7 = (bf16[1024,128]{1,0:T(8,128)(2,1)S(1)}, bf16[1024,128]{1,0:T(8,128)(2,1)}, u32[]{:S(2)}) copy-start(bf16[1024,128]{1,0:T(8,128)(2,1)} %param.18) | copy-start | bytes 786436
  57.2 4.0 %copy-start.8 = (bf16[128,1024]{1,0:T(8,128)(2,1)S(1)}, bf16[128,1024]{1,0:T(8,128)(2,1)}, u32[]{:S(2)}) copy-start(bf16[128,1024]{1,0:T(8,128)(2,1)} %param.19) | copy-start | bytes 786436
  61.4 1.6 %copy-start.4 = (bf16[1,3072,128]{2,1,0:T(8,128)(2,1)S(1)}, bf16[1,3072,128]{2,1,0:T(8,128)(2,1)}, u32[]{:S(2)}) copy-start(bf16[1,3072,128]{2,1,0:T(8,128)(2,1)} %param.20) | copy-start | bytes 2359300
  62.9 1.7 %copy-start.1 = (bf16[8,200,1024]{2,1,0:T(8,128)(2,1)}, bf16[8,200,1024]{2,1,0:T(8,128)(2,1)S(1)}, u32[]{:S(2)}) copy-start(bf16[8,200,1024]{2,1,0:T(8,128)(2,1)S(1)} %get-tuple-element.3) | copy-start | bytes 9830404
  62.9 3.1 %copy-start.6 = (bf16[1,128,1024]{2,1,0:T(8,128)(2,1)S(1)}, bf16[1,128,1024]{2,1,0:T(8,128)(2,1)}, u32[]{:S(2)}) copy-start(bf16[1,128,1024]{2,1,0:T(8,128)(2,1)} %param.21) | copy-start | bytes 786436
  72.5 8.5 %copy-start.2 = (bf16[8,200,1024]{2,1,0:T(8,128)(2,1)S(1)}, bf16[8,200,1024]{2,1,0:T(8,128)(2,1)}, u32[]{:S(2)}) copy-start(bf16[8,200,1024]{2,1,0:T(8,128)(2,1)} %copy-done.1) | copy-start | bytes 9830404
  81.0 1.3 %copy-start.5 = (bf16[1,2048,192]{1,2,0:T(8,128)(2,1)S(1)}, bf16[1,2048,192]{1,2,0:T(8,128)(2,1)}, u32[]{:S(2)}) copy-start(bf16[1,2048,192]{1,2,0:T(8,128)(2,1)} %param.22) | copy-start | bytes 2359300
  81.1 1.6 %copy-start.9 = (bf16[1,192,107]{2,1,0:T(8,128)(2,1)S(1)}, bf16[1,192,107]{2,1,0:T(8,128)(2,1)}, u32[]{:S(2)}) copy-start(bf16[1,192,107]{2,1,0:T(8,128)(2,1)} %param.23) | copy-start | bytes 123268
  83.6 7.8 %all-to-all-start.2 = ((f32[8,1,107]{2,1,0:T(1,128)}), f32[8,1,107]{2,1,0:T(1,128)S(1)}, u32[]{:S(2)}, u32[]{:S(2)}) async-start(f32[8,1,107]{2,1,0:T(1,128)} %bitcast.33), calls=%async_computation.2 | async-start | bytes 8192 | tf_op jit(solution)/shard_map/all_to_all | solution.py:179
  91.5 8.0 %all-to-all-start.3 = ((f32[8,1,192]{2,1,0:T(1,128)}), f32[8,1,192]{2,1,0:T(1,128)S(1)}, u32[]{:S(2)}, u32[]{:S(2)}) async-start(f32[8,1,192]{2,1,0:T(1,128)} %copy.25), calls=%async_computation.3 | async-start | bytes 16384 | tf_op jit(solution)/shard_map/all_to_all | solution.py:178
where the time goes:
time: 115 us; the launch traced here: 114 us
  matrix products  35.4 us (31%)
  other arithmetic  22.1 us (19%)
  starting transfers between devices  15.2 us (13%)
  waiting for transfers between devices  14.9 us (13%)
  blocking collectives  13.4 us (12%)
  local copies, waits for them, and re-layouts  11.9 us (10%)
    all_gather x1, blocking collectives, shards(): lax.all_gather(normed, 'mem', axis=0, tiled=True)  13.4 us
    dot_general x7, matrix products, trunk(): jnp.einsum('nfk,kc->nfc', stacked_rows, branch_weight[branch - 1], prefer...  11.8 us
    div x1, other arithmetic, head(): weights = weights / jnp.sum(weights, axis=0)  8.48 us
    convert_element_type x6, other arithmetic, trunk(): present_frames = (present_frames.astype(jnp.float32) + previous.astype(jn...  6.68 us
    dot_general x1, matrix products, head(): jnp.dot(attended, score_weight, preferred_element_type=jnp.float32)  6.53 us
    all_to_all x1, waiting for transfers between devices, shards(): lax.all_to_all(outbound, 'grp', split_axis=0, concat_axis=0, tiled=True)  6.24 us
    all_to_all x1, starting transfers between devices, shards(): lax.all_to_all(send_flags.astype(jnp.bfloat16), 'grp', split_axis=0, conc...  5.17 us
    dot_general x1, matrix products, trunk(): jnp.einsum('nfk,kc->nfc', front_out, expand_weight, preferred_element_typ...  3.96 us
  transfers between devices with their start and end apart: 4, of which 4 were waited for; matrix products, arithmetic and copies ran while one was open for 5% of the time, Pallas kernels for 0%

commit v1 on v0

v1 whole, which is shorter than its diff:
```python
import functools

import jax
import jax.numpy as jnp
from jax import lax
from jax.experimental import pallas as pl
from jax.experimental.pallas import tpu as pltpu
from jax.sharding import PartitionSpec as P

MELS = 80
SCALE = 8
FRAMES = 200
LANES = 128
FLAT_ROWS = 125
SEND_ROWS = 128
LEAD = 8
SLOT_ROWS = LEAD + SEND_ROWS
TAPS0 = 5
WINDOW = 512
TILE = 400
EPS_STAT = 1e-05
EPS_NORM = 1e-06

MESH = pl.DeviceIdType.MESH
F32 = jnp.float32
BF16 = jnp.bfloat16


def dot(a, b):
    return jnp.dot(a, b, preferred_element_type=F32)


def dot_split(values, weight):
    rows = values.shape[0]
    high = values.astype(BF16).astype(F32)
    both = jnp.concatenate([high, values - high], axis=0).astype(BF16)
    product = dot(both, weight)
    return product[:rows] + product[rows:]


def kernel(
    groups,
    members,
    bank_hbm,
    dest_ref,
    w0_hbm,
    expand_hbm,
    branch_hbm,
    merge_hbm,
    squeeze_hbm,
    excite_hbm,
    attend_hbm,
    score_hbm,
    embed_hbm,
    lang_hbm,
    logits_ref,
    sim_ref,
    bank,
    w0,
    expand,
    branch,
    merge,
    squeeze,
    excite,
    attend,
    score,
    embed,
    lang,
    staged,
    outbox,
    arrived,
    slots,
    cols,
    front,
    work,
    wide,
    ping,
    pong,
    attn,
    back,
    home,
    own,
    normed,
    gathered,
    load_sem,
    out_send,
    out_recv,
    back_send,
    back_recv,
    mem_send,
    mem_recv,
):
    stored = bank.shape[0]
    rows_all = FRAMES * groups
    tiles = rows_all // TILE
    tile_frames = TILE // groups
    channels = front.shape[1]
    me = lax.axis_index("grp")
    my_mem = lax.axis_index("mem")

    pairs = [
        (bank_hbm, bank),
        (w0_hbm, w0.at[pl.ds(0, w0_hbm.shape[0])]),
        (expand_hbm, expand),
        (branch_hbm, branch),
        (merge_hbm, merge),
        (squeeze_hbm, squeeze),
        (excite_hbm, excite),
        (attend_hbm, attend),
        (score_hbm, score),
        (embed_hbm, embed),
        (lang_hbm, lang),
    ]
    loads = [
        pltpu.make_async_copy(source, target, load_sem.at[i])
        for i, (source, target) in enumerate(pairs)
    ]
    for load in loads:
        load.start()

    barrier = pltpu.get_barrier_semaphore()
    for step in range(1, groups):
        pl.semaphore_signal(
            barrier, inc=1, device_id=(lax.rem(me + step, groups), my_mem), device_id_type=MESH
        )
    for step in range(1, members):
        pl.semaphore_signal(
            barrier, inc=1, device_id=(me, lax.rem(my_mem + step, members)), device_id_type=MESH
        )

    staged[...] = jnp.zeros_like(staged)
    slots[...] = jnp.zeros_like(slots)
    w0[w0_hbm.shape[0] :, :] = jnp.zeros((WINDOW - w0_hbm.shape[0], channels), BF16)
    halo = 2 * groups
    for buffer in (ping, pong):
        buffer[:halo, :] = jnp.zeros((halo, LANES), BF16)
        buffer[halo + rows_all :, :] = jnp.zeros((halo, LANES), BF16)
    back[...] = jnp.zeros_like(back)

    loads[0].wait()
    for row in range(FLAT_ROWS):
        staged[pl.ds(row, stored, stride=SEND_ROWS), :] = bank[:, row * LANES : (row + 1) * LANES]

    pl.semaphore_wait(barrier, groups - 1 + members - 1)

    def segment_for(group):
        picked = jnp.zeros((SEND_ROWS, LANES), F32)
        for s in range(stored):
            rows = staged[s * SEND_ROWS : (s + 1) * SEND_ROWS, :]
            picked = jnp.where(dest_ref[0, s] == group, rows, picked)
        return picked.astype(BF16)

    sends = []
    for step in range(1, groups):
        group = lax.rem(me + step, groups)
        outbox[step] = segment_for(group)
        copy = pltpu.make_async_remote_copy(
            src_ref=outbox.at[step],
            dst_ref=arrived.at[me],
            send_sem=out_send.at[step],
            recv_sem=out_recv.at[me],
            device_id=(group, my_mem),
            device_id_type=MESH,
        )
        copy.start()
        sends.append(copy)
    arrived[me] = segment_for(me)

    def place(slot):
        start = pl.multiple_of(slot * SLOT_ROWS + LEAD, 8)
        slots[pl.ds(start, SEND_ROWS), :] = arrived[slot].astype(F32)

    place(me)
    for step in range(1, groups):
        source = lax.rem(me + groups - step, groups)
        pltpu.make_async_remote_copy(
            src_ref=outbox.at[step],
            dst_ref=arrived.at[source],
            send_sem=out_send.at[step],
            recv_sem=out_recv.at[source],
            device_id=(source, my_mem),
            device_id_type=MESH,
        ).wait_recv()
        place(source)

    lane = lax.broadcasted_iota(jnp.int32, (groups, LANES), 1)

    def windows(block, _):
        first = block * 5
        held = {}

        def row_at(index):
            if index not in held:
                held[index] = slots[pl.ds(first + index, groups, stride=SLOT_ROWS), :]
            return held[index]

        pair = []
        for phase in range(8):
            begin = phase * MELS + LEAD * LANES - 2 * MELS
            index, offset = begin // LANES, begin % LANES
            pieces = []
            for j in range(4):
                low = row_at(index + j)
                if offset:
                    high = row_at(index + j + 1) if j < 3 else None
                    low = pltpu.roll(low, LANES - offset, 1)
                    if high is not None:
                        high = pltpu.roll(high, LANES - offset, 1)
                        low = jnp.where(lane < LANES - offset, low, high)
                if j == 3:
                    low = jnp.where(lane < TAPS0 * MELS - 3 * LANES, low, 0.0)
                pieces.append(low)
            pair.append(jnp.concatenate(pieces, axis=1))
            if len(pair) == 2:
                start = pl.multiple_of((block * 8 + phase - 1) * groups, 16)
                cols[pl.ds(start, 2 * groups), :] = jnp.concatenate(pair, axis=0).astype(BF16)
                pair = []
        return 0

    lax.fori_loop(0, FRAMES // 8, windows, 0)

    loads[1].wait()
    loads[2].wait()

    def first_layers(tile, _):
        start = pl.multiple_of(tile * TILE, 16)
        rows = pl.ds(start, TILE)
        out = jnp.maximum(dot(cols[rows, :], w0[...]), 0.0).astype(BF16)
        front[rows, :] = out
        expanded = jnp.maximum(dot(out, expand[...]), 0.0).astype(BF16)
        work[rows, :] = expanded
        ping[pl.ds(start + halo, TILE), :] = expanded[:, LANES : 2 * LANES]
        return 0

    lax.fori_loop(0, tiles, first_layers, 0)

    loads[3].wait()
    buffers = (ping, pong)
    for i in range(1, SCALE):
        source, target = buffers[(i - 1) % 2], buffers[i % 2]

        def one_branch(tile, _, i=i, source=source, target=target):
            start = pl.multiple_of(tile * 2 * TILE, 16)
            rows = pl.ds(start, 2 * TILE)
            stacked = jnp.concatenate(
                [source[pl.ds(start + k * halo, 2 * TILE), :] for k in range(3)], axis=1
            )
            out = jnp.maximum(dot(stacked, branch[i - 1]), 0.0).astype(BF16)
            work[rows, i * LANES : (i + 1) * LANES] = out
            if i < SCALE - 1:
                following = work[rows, (i + 1) * LANES : (i + 2) * LANES].astype(F32)
                target[pl.ds(start + halo, 2 * TILE), :] = (following + out.astype(F32)).astype(BF16)
            return 0

        lax.fori_loop(0, tiles // 2, one_branch, 0, unroll=True)

    loads[4].wait()

    def by_frame(values):
        return values.reshape(tile_frames, groups, values.shape[1])

    def merging(tile, total):
        rows = pl.ds(pl.multiple_of(tile * TILE, 16), TILE)
        merged = jnp.maximum(dot(work[rows, :], merge[...]), 0.0)
        wide[rows, :] = merged
        return total + jnp.sum(by_frame(merged), axis=0)

    zeros = jnp.zeros((groups, channels), F32)
    total = lax.fori_loop(0, tiles, merging, zeros)

    loads[5].wait()
    loads[6].wait()
    hidden = jnp.maximum(dot_split(total / FRAMES, squeeze[...]), 0.0)
    excited = 1.0 / (1.0 + jnp.exp(-dot_split(hidden, excite[...])))

    loads[7].wait()
    pivot = front[0 : 2 * groups, :].astype(F32)[:groups] + wide[0:groups, :] * excited

    def trunk_out(tile, carry):
        first, second = carry
        rows = pl.ds(pl.multiple_of(tile * TILE, 16), TILE)
        out = by_frame(front[rows, :].astype(F32)) + by_frame(wide[rows, :]) * excited
        out = out.reshape(TILE, channels).astype(BF16)
        work[rows, :] = out
        attn[rows, :] = dot(out, attend[0:channels, :])
        moved = by_frame(out.astype(F32)) - pivot
        return first + jnp.sum(moved, axis=0), second + jnp.sum(moved * moved, axis=0)

    first, second = lax.fori_loop(0, tiles, trunk_out, (zeros, zeros))
    shift = first / FRAMES
    center = pivot + shift
    spread = jnp.sqrt(jnp.maximum(second / FRAMES - shift * shift, 0.0) + EPS_STAT)
    context = dot_split(center, attend[channels : 2 * channels, :]) + dot_split(
        spread, attend[2 * channels :, :]
    )

    loads[8].wait()

    def energies(tile, total):
        rows = pl.ds(pl.multiple_of(tile * TILE, 16), TILE)
        attended = jnp.tanh(by_frame(attn[rows, :]) + context).reshape(TILE, -1).astype(BF16)
        weights = jnp.exp(dot(attended, score[...]))
        wide[rows, :] = weights
        return total + jnp.sum(by_frame(weights), axis=0)

    scale = 1.0 / lax.fori_loop(0, tiles, energies, zeros)

    def weighted(tile, total):
        rows = pl.ds(pl.multiple_of(tile * TILE, 16), TILE)
        weights = by_frame(wide[rows, :]) * scale
        return total + jnp.sum(weights * by_frame(work[rows, :].astype(F32)), axis=0)

    mean = lax.fori_loop(0, tiles, weighted, zeros)

    def deviating(tile, total):
        rows = pl.ds(pl.multiple_of(tile * TILE, 16), TILE)
        weights = by_frame(wide[rows, :]) * scale
        moved = by_frame(work[rows, :].astype(F32)) - mean
        return total + jnp.sum(weights * (moved * moved), axis=0)

    deviation = jnp.sqrt(lax.fori_loop(0, tiles, deviating, zeros) + EPS_STAT)

    loads[9].wait()
    loads[10].wait()
    pooled = jnp.concatenate([mean, deviation], axis=1).astype(BF16)
    embedding = dot(pooled, embed[...])
    scores = dot(embedding.astype(BF16), lang[...])
    width = embedding.shape[1]
    langs = scores.shape[1]
    back[:, 0, :] = embedding[:, :LANES]
    back[:, 1, : width - LANES] = embedding[:, LANES:]
    back[:, 2, :langs] = scores

    for step in range(1, groups):
        group = lax.rem(me + step, groups)
        copy = pltpu.make_async_remote_copy(
            src_ref=back.at[group],
            dst_ref=home.at[me],
            send_sem=back_send.at[step],
            recv_sem=back_recv.at[me],
            device_id=(group, my_mem),
            device_id_type=MESH,
        )
        copy.start()
        sends.append(copy)
    home[me] = back[me]
    for step in range(1, groups):
        source = lax.rem(me + groups - step, groups)
        pltpu.make_async_remote_copy(
            src_ref=back.at[source],
            dst_ref=home.at[source],
            send_sem=back_send.at[step],
            recv_sem=back_recv.at[source],
            device_id=(source, my_mem),
            device_id_type=MESH,
        ).wait_recv()
    for s in range(stored):
        picked = home[0]
        for group in range(1, groups):
            picked = jnp.where(dest_ref[0, s] == group, home[group], picked)
        own[s] = picked

    left, right = own[:, 0, :], own[:, 1, :]
    logits_ref[...] = own[:, 2, :][:, :langs]
    squares = jnp.sum(left * left + right * right, axis=1, keepdims=True)
    factor = lax.rsqrt(squares / width + EPS_NORM)
    mine = jnp.concatenate([left * factor, right * factor], axis=1).astype(BF16)
    normed[...] = mine.astype(F32)
    for step in range(1, members):
        member = lax.rem(my_mem + step, members)
        copy = pltpu.make_async_remote_copy(
            src_ref=normed,
            dst_ref=gathered.at[my_mem],
            send_sem=mem_send.at[step],
            recv_sem=mem_recv.at[my_mem],
            device_id=(me, member),
            device_id_type=MESH,
        )
        copy.start()
        sends.append(copy)
    gathered[my_mem] = normed[...]
    for step in range(1, members):
        source = lax.rem(my_mem + members - step, members)
        pltpu.make_async_remote_copy(
            src_ref=normed,
            dst_ref=gathered.at[source],
            send_sem=mem_send.at[step],
            recv_sem=mem_recv.at[source],
            device_id=(me, source),
            device_id_type=MESH,
        ).wait_recv()
    every = gathered[...].reshape(members * stored, 2 * LANES).astype(BF16)
    sim_ref[...] = (
        lax.dot_general(mine, every, (((1,), (1,)), ((), ())), preferred_element_type=F32) / width
    )
    for copy in sends:
        copy.wait_send()


def shards(
    filterbank,
    destination,
    initial_conv_weight,
    expand_weight,
    branch_weight,
    merge_weight,
    squeeze_weight,
    excite_weight,
    attend_weight,
    score_weight,
    embed_weight,
    language_weight,
):
    groups = lax.axis_size("grp")
    members = lax.axis_size("mem")
    stored = filterbank.shape[2]
    rows = FRAMES * groups
    channels = expand_weight.shape[0]
    langs = language_weight.shape[2]
    operands = (
        filterbank.reshape(stored, FRAMES * MELS),
        destination,
        initial_conv_weight,
        expand_weight,
        branch_weight,
        merge_weight,
        squeeze_weight,
        excite_weight,
        attend_weight[0],
        score_weight[0],
        embed_weight[0],
        language_weight[0],
    )
    copied = [pltpu.VMEM(a.shape, a.dtype) for a in operands]
    del copied[1]
    copied[1] = pltpu.VMEM((WINDOW, channels), BF16)
    anywhere = pl.BlockSpec(memory_space=pl.ANY)
    in_specs = [anywhere] * len(operands)
    in_specs[1] = pl.BlockSpec(memory_space=pltpu.SMEM)
    dma = pltpu.SemaphoreType.DMA
    logits, similarity = pl.pallas_call(
        functools.partial(kernel, groups, members),
        out_shape=(
            jax.ShapeDtypeStruct((stored, langs), F32),
            jax.ShapeDtypeStruct((stored, members * stored), F32),
        ),
        in_specs=in_specs,
        out_specs=[pl.BlockSpec(memory_space=pltpu.VMEM)] * 2,
        scratch_shapes=copied
        + [
            pltpu.VMEM((stored * SEND_ROWS, LANES), F32),
            pltpu.VMEM((groups, SEND_ROWS, LANES), BF16),
            pltpu.VMEM((groups, SEND_ROWS, LANES), BF16),
            pltpu.VMEM((groups * SLOT_ROWS, LANES), F32),
            pltpu.VMEM((rows, WINDOW), BF16),
            pltpu.VMEM((rows, channels), BF16),
            pltpu.VMEM((rows, channels), BF16),
            pltpu.VMEM((rows, channels), F32),
            pltpu.VMEM((rows + 4 * groups, LANES), BF16),
            pltpu.VMEM((rows + 4 * groups, LANES), BF16),
            pltpu.VMEM((rows, LANES), F32),
            pltpu.VMEM((groups, 8, LANES), F32),
            pltpu.VMEM((groups, 8, LANES), F32),
            pltpu.VMEM((stored, 8, LANES), F32),
            pltpu.VMEM((stored, 2 * LANES), F32),
            pltpu.VMEM((members, stored, 2 * LANES), F32),
            dma((len(copied),)),
            dma((groups,)),
            dma((groups,)),
            dma((groups,)),
            dma((groups,)),
            dma((members,)),
            dma((members,)),
        ],
        compiler_params=pltpu.CompilerParams(
            collective_id=0, has_side_effects=True, vmem_limit_bytes=60 * 1024 * 1024
        ),
        cost_estimate=pl.CostEstimate(
            flops=rows * 12_000_000, bytes_accessed=10_000_000, transcendentals=rows * 1200
        ),
    )(*operands)
    return (logits[None], similarity[None])


def solution(mesh):
    return jax.shard_map(
        shards,
        mesh=mesh,
        in_specs=(
            P("grp", "mem", None, None),
            P("grp", "mem"),
            P(),
            P(),
            P(),
            P(),
            P(),
            P(),
            P("grp", None, None),
            P("grp", None, None),
            P("grp", None, None),
            P("grp", None, None),
        ),
        out_specs=(P("grp", "mem", None), P("grp", "mem", None)),
        check_vma=False,
    )
```

time: 115 us -> 48.5 us (0.42)
  Pallas kernels: 0 us -> 42.8 us
  matrix products: 35.4 us -> 0 us
  other arithmetic: 22.1 us -> 0 us
  starting transfers between devices: 15.2 us -> 0 us
  waiting for transfers between devices: 14.9 us -> 0 us
  blocking collectives: 13.4 us -> 0 us
  local copies, waits for them, and re-layouts: 11.9 us -> 4.77 us
    pallas_call x0 -> x1, Pallas kernels: none -> 42.8 us  [shards(): pl.pallas_call(functools.partial(kernel, groups, members), out_shape=(jax...]
    dot_general x24 -> x0, matrix products: 35.4 us -> none  [the longest x7 11.8 us: trunk(): jnp.einsum('nfk,kc->nfc', stacked_rows, branch_weight[branch - 1], prefer...]
    all_to_all x4 -> x0, starting transfers between devices: 15.2 us -> none  [the longest x1 5.17 us: shards(): lax.all_to_all(send_flags.astype(jnp.bfloat16), 'grp', split_axis=0, conc...]
    all_to_all x4 -> x0, waiting for transfers between devices: 14.9 us -> none  [the longest x1 6.24 us: shards(): lax.all_to_all(outbound, 'grp', split_axis=0, concat_axis=0, tiled=True)]
    all_gather x1 -> x0, blocking collectives: 13.4 us -> none  [shards(): lax.all_gather(normed, 'mem', axis=0, tiled=True)]
    div x2 -> x0, other arithmetic: 8.49 us -> none  [the longest x1 8.48 us: head(): weights = weights / jnp.sum(weights, axis=0)]
    convert_element_type x8 -> x0, other arithmetic: 6.89 us -> none  [the longest x6 6.68 us: trunk(): present_frames = (present_frames.astype(jnp.float32) + previous.astype(jn...]
    reduce_sum x5 -> x0, other arithmetic: 4.8 us -> none  [the longest x1 1.51 us: head(): center = jnp.mean(widened, axis=0)]
  transfers between devices with their start and end apart: 4 -> 0, of which waited for: 4 -> 0; matrix products, arithmetic and copies ran while one was open for 5% -> 0% of each run, Pallas kernels for 0% -> 0%
where the time goes in v1:
time: 48.5 us; the launch traced here: 48.2 us
  Pallas kernels  42.8 us (88%)
  local copies, waits for them, and re-layouts  4.77 us (10%)
  between operations  0.64 us (1%)
    pallas_call x1, Pallas kernels, shards(): pl.pallas_call(functools.partial(kernel, groups, members), out_shape=(jax...  42.8 us
    unnamed x3, local copies, waits for them, and re-layouts  4.77 us

profile of v1, /device:TPU:0, one launch (start us, length us, event | category | flops | bytes accessed | tf_op | source)
XLA Modules:
  0.0 48.2 jit_solution(4435678331250610852)
XLA Ops:
  0.6 2.2 %copy.14 = bf16[1,2048,192]{2,1,0:T(8,128)(2,1)} copy(bf16[1,2048,192]{1,2,0:T(8,128)(2,1)} %param.22) | data formatting | bytes 1572864 | tf_op args[10]
  2.9 42.8 %shard_map.131 = (f32[8,107]{1,0:T(8,128)}, f32[8,32]{1,0:T(8,128)}) custom-call(f32[8,16000]{1,0:T(8,128)} %bitcast.11, s32[1,8]{1,0:T(1,128)} %dest_ref.1, bf16[400,1024]{1,0:T(8,128)(2,1)} %w0_hbm.1, bf16[1024,1024]{1,0:T(8,128)(2,1)} %expand_hbm.1, bf16[7,384,128]{2,1,0:T(8,128)(2,1)} %branch_hbm.1, bf16[1024,1024]{1,0:T(8,128)(2,1)} %merge_hbm.1, ...), custom_call_target="tpu_custom_call" | custom-call | flops 19200000000 | bytes 10000000 | tf_op jit(solution)/shard_map/pallas_call | solution.py:441
  45.7 1.3 %copy.17 = f32[1,8,107]{2,1,0:T(8,128)} copy(f32[1,8,107]{2,1,0:T(8,128)} %bitcast.9) | data formatting | bytes 6848
  47.0 1.3 %copy.18 = f32[1,8,32]{2,1,0:T(8,128)} copy(f32[1,8,32]{2,1,0:T(8,128)} %bitcast.8) | data formatting | bytes 2048

commit v2 on v1

--- a/solution.py
+++ b/solution.py
@@ -18,6 +18,7 @@
 TAPS0 = 5
 WINDOW = 512
 TILE = 400
+CHUNK = 256
 EPS_STAT = 1e-05
 EPS_NORM = 1e-06
 
@@ -53,8 +54,7 @@
     score_hbm,
     embed_hbm,
     lang_hbm,
-    logits_ref,
-    sim_ref,
+    result_ref,
     bank,
     w0,
     expand,
@@ -102,7 +102,8 @@
         (bank_hbm, bank),
         (w0_hbm, w0.at[pl.ds(0, w0_hbm.shape[0])]),
         (expand_hbm, expand),
-        (branch_hbm, branch),
+        (branch_hbm, branch.at[:, pl.ds(0, 3 * LANES), pl.ds(0, LANES)]),
+        (branch_hbm, branch.at[:, pl.ds(LANES, 3 * LANES), pl.ds(LANES, LANES)]),
         (merge_hbm, merge),
         (squeeze_hbm, squeeze),
         (excite_hbm, excite),
@@ -132,16 +133,18 @@
     slots[...] = jnp.zeros_like(slots)
     w0[w0_hbm.shape[0] :, :] = jnp.zeros((WINDOW - w0_hbm.shape[0], channels), BF16)
     halo = 2 * groups
+    half = rows_all // 2
     for buffer in (ping, pong):
-        buffer[:halo, :] = jnp.zeros((halo, LANES), BF16)
-        buffer[halo + rows_all :, :] = jnp.zeros((halo, LANES), BF16)
+        buffer[0, half:, :] = jnp.zeros((halo, LANES), BF16)
+        buffer[1, :halo, :] = jnp.zeros((halo, LANES), BF16)
+    empty = jnp.zeros((SCALE - 1, LANES, LANES), BF16)
+    branch[:, 3 * LANES :, :LANES] = empty
+    branch[:, :LANES, LANES:] = empty
     back[...] = jnp.zeros_like(back)
 
     loads[0].wait()
     for row in range(FLAT_ROWS):
         staged[pl.ds(row, stored, stride=SEND_ROWS), :] = bank[:, row * LANES : (row + 1) * LANES]
-
-    pl.semaphore_wait(barrier, groups - 1 + members - 1)
 
     def segment_for(group):
         picked = jnp.zeros((SEND_ROWS, LANES), F32)
@@ -150,10 +153,14 @@
             picked = jnp.where(dest_ref[0, s] == group, rows, picked)
         return picked.astype(BF16)
 
+    for step in range(1, groups):
+        outbox[step] = segment_for(lax.rem(me + step, groups))
+
+    pl.semaphore_wait(barrier, groups - 1 + members - 1)
+
     sends = []
     for step in range(1, groups):
         group = lax.rem(me + step, groups)
-        outbox[step] = segment_for(group)
         copy = pltpu.make_async_remote_copy(
             src_ref=outbox.at[step],
             dst_ref=arrived.at[me],
@@ -212,7 +219,8 @@
                 pieces.append(low)
             pair.append(jnp.concatenate(pieces, axis=1))
             if len(pair) == 2:
-                start = pl.multiple_of((block * 8 + phase - 1) * groups, 16)
+                side, place_in = phase // 2 % 2, phase // 4
+                start = pl.multiple_of(side * half + (block * 2 + place_in) * halo, 16)
                 cols[pl.ds(start, 2 * groups), :] = jnp.concatenate(pair, axis=0).astype(BF16)
                 pair = []
         return 0
@@ -222,69 +230,88 @@
     loads[1].wait()
     loads[2].wait()
 
+    chunks = [slice(c, c + CHUNK) for c in range(0, channels, CHUNK)]
+    half_tiles = tiles // 2
+
     def first_layers(tile, _):
-        start = pl.multiple_of(tile * TILE, 16)
-        rows = pl.ds(start, TILE)
-        out = jnp.maximum(dot(cols[rows, :], w0[...]), 0.0).astype(BF16)
-        front[rows, :] = out
-        expanded = jnp.maximum(dot(out, expand[...]), 0.0).astype(BF16)
-        work[rows, :] = expanded
-        ping[pl.ds(start + halo, TILE), :] = expanded[:, LANES : 2 * LANES]
+        rows = pl.ds(pl.multiple_of(tile * TILE, 16), TILE)
+        for chunk in chunks:
+            out = jnp.maximum(dot(cols[rows, :], w0[:, chunk]), 0.0)
+            front[rows, chunk] = out.astype(BF16)
+        side = tile // half_tiles
+        start = pl.multiple_of(tile % half_tiles * TILE + side * halo, 16)
+        for chunk in chunks:
+            expanded = jnp.maximum(dot(front[rows, :], expand[:, chunk]), 0.0).astype(BF16)
+            work[rows, chunk] = expanded
+            if chunk.start == 0:
+                ping[side, pl.ds(start, TILE), :] = expanded[:, LANES : 2 * LANES]
         return 0
 
     lax.fori_loop(0, tiles, first_layers, 0)
 
     loads[3].wait()
+    loads[4].wait()
     buffers = (ping, pong)
     for i in range(1, SCALE):
         source, target = buffers[(i - 1) % 2], buffers[i % 2]
 
         def one_branch(tile, _, i=i, source=source, target=target):
-            start = pl.multiple_of(tile * 2 * TILE, 16)
-            rows = pl.ds(start, 2 * TILE)
-            stacked = jnp.concatenate(
-                [source[pl.ds(start + k * halo, 2 * TILE), :] for k in range(3)], axis=1
+            start = pl.multiple_of(tile * TILE, 16)
+            near, far = pl.ds(start, TILE), pl.ds(start + halo, TILE)
+            window = jnp.concatenate(
+                [source[1, near, :], source[0, near, :], source[1, far, :], source[0, far, :]], axis=1
             )
-            out = jnp.maximum(dot(stacked, branch[i - 1]), 0.0).astype(BF16)
-            work[rows, i * LANES : (i + 1) * LANES] = out
-            if i < SCALE - 1:
-                following = work[rows, (i + 1) * LANES : (i + 2) * LANES].astype(F32)
-                target[pl.ds(start + halo, 2 * TILE), :] = (following + out.astype(F32)).astype(BF16)
+            out = jnp.maximum(dot(window, branch[i - 1]), 0.0).astype(BF16)
+            for side, spot in ((0, near), (1, far)):
+                rows = pl.ds(start + side * half, TILE)
+                mine = out[:, side * LANES : (side + 1) * LANES]
+                work[rows, i * LANES : (i + 1) * LANES] = mine
+                if i < SCALE - 1:
+                    following = work[rows, (i + 1) * LANES : (i + 2) * LANES].astype(F32)
+                    target[side, spot, :] = (following + mine.astype(F32)).astype(BF16)
             return 0
 
-        lax.fori_loop(0, tiles // 2, one_branch, 0, unroll=True)
-
-    loads[4].wait()
+        lax.fori_loop(0, half_tiles, one_branch, 0, unroll=True)
+
+    loads[5].wait()
 
     def by_frame(values):
         return values.reshape(tile_frames, groups, values.shape[1])
 
     def merging(tile, total):
         rows = pl.ds(pl.multiple_of(tile * TILE, 16), TILE)
-        merged = jnp.maximum(dot(work[rows, :], merge[...]), 0.0)
-        wide[rows, :] = merged
-        return total + jnp.sum(by_frame(merged), axis=0)
+        sums = []
+        for chunk in chunks:
+            merged = jnp.maximum(dot(work[rows, :], merge[:, chunk]), 0.0)
+            wide[rows, chunk] = merged
+            sums.append(jnp.sum(by_frame(merged), axis=0))
+        return total + jnp.concatenate(sums, axis=1)
 
     zeros = jnp.zeros((groups, channels), F32)
     total = lax.fori_loop(0, tiles, merging, zeros)
 
-    loads[5].wait()
     loads[6].wait()
+    loads[7].wait()
     hidden = jnp.maximum(dot_split(total / FRAMES, squeeze[...]), 0.0)
     excited = 1.0 / (1.0 + jnp.exp(-dot_split(hidden, excite[...])))
 
-    loads[7].wait()
+    loads[8].wait()
     pivot = front[0 : 2 * groups, :].astype(F32)[:groups] + wide[0:groups, :] * excited
 
     def trunk_out(tile, carry):
         first, second = carry
         rows = pl.ds(pl.multiple_of(tile * TILE, 16), TILE)
-        out = by_frame(front[rows, :].astype(F32)) + by_frame(wide[rows, :]) * excited
-        out = out.reshape(TILE, channels).astype(BF16)
-        work[rows, :] = out
-        attn[rows, :] = dot(out, attend[0:channels, :])
-        moved = by_frame(out.astype(F32)) - pivot
-        return first + jnp.sum(moved, axis=0), second + jnp.sum(moved * moved, axis=0)
+        sums, squares = [], []
+        for chunk in chunks:
+            out = by_frame(wide[rows, chunk]) * excited[:, chunk]
+            out = by_frame(front[rows, chunk].astype(F32)) + out
+            out = out.reshape(TILE, CHUNK).astype(BF16)
+            work[rows, chunk] = out
+            moved = by_frame(out.astype(F32)) - pivot[:, chunk]
+            sums.append(jnp.sum(moved, axis=0))
+            squares.append(jnp.sum(moved * moved, axis=0))
+        attn[rows, :] = dot(work[rows, :], attend[0:channels, :])
+        return first + jnp.concatenate(sums, axis=1), second + jnp.concatenate(squares, axis=1)
 
     first, second = lax.fori_loop(0, tiles, trunk_out, (zeros, zeros))
     shift = first / FRAMES
@@ -294,36 +321,36 @@
         spread, attend[2 * channels :, :]
     )
 
-    loads[8].wait()
-
-    def energies(tile, total):
+    loads[9].wait()
+
+    inverse = 1.0 / spread
+
+    def energies(tile, carry):
         rows = pl.ds(pl.multiple_of(tile * TILE, 16), TILE)
         attended = jnp.tanh(by_frame(attn[rows, :]) + context).reshape(TILE, -1).astype(BF16)
-        weights = jnp.exp(dot(attended, score[...]))
-        wide[rows, :] = weights
-        return total + jnp.sum(by_frame(weights), axis=0)
-
-    scale = 1.0 / lax.fori_loop(0, tiles, energies, zeros)
-
-    def weighted(tile, total):
-        rows = pl.ds(pl.multiple_of(tile * TILE, 16), TILE)
-        weights = by_frame(wide[rows, :]) * scale
-        return total + jnp.sum(weights * by_frame(work[rows, :].astype(F32)), axis=0)
-
-    mean = lax.fori_loop(0, tiles, weighted, zeros)
-
-    def deviating(tile, total):
-        rows = pl.ds(pl.multiple_of(tile * TILE, 16), TILE)
-        weights = by_frame(wide[rows, :]) * scale
-        moved = by_frame(work[rows, :].astype(F32)) - mean
-        return total + jnp.sum(weights * (moved * moved), axis=0)
-
-    deviation = jnp.sqrt(lax.fori_loop(0, tiles, deviating, zeros) + EPS_STAT)
-
-    loads[9].wait()
+        parts = ([], [], [])
+        for chunk in chunks:
+            weights = by_frame(jnp.exp(dot(attended, score[:, chunk])))
+            value = by_frame(work[rows, chunk].astype(F32))
+            value = (value - center[:, chunk]) * inverse[:, chunk]
+            parts[0].append(jnp.sum(weights, axis=0))
+            weights = weights * value
+            parts[1].append(jnp.sum(weights, axis=0))
+            parts[2].append(jnp.sum(weights * value, axis=0))
+        return tuple(c + jnp.concatenate(p, axis=1) for c, p in zip(carry, parts))
+
+    norm, weighted, squared = lax.fori_loop(0, tiles, energies, (zeros, zeros, zeros))
+    weighted = weighted / norm
+    squared = jnp.maximum(squared / norm - weighted * weighted, 0.0)
+    mean = center + spread * weighted
+    deviation = jnp.sqrt(spread * spread * squared + EPS_STAT)
+
     loads[10].wait()
+    loads[11].wait()
     pooled = jnp.concatenate([mean, deviation], axis=1).astype(BF16)
-    embedding = dot(pooled, embed[...])
+    embedding = lax.dot_general(
+        pooled, embed[...], (((1,), (1,)), ((), ())), preferred_element_type=F32
+    )
     scores = dot(embedding.astype(BF16), lang[...])
     width = embedding.shape[1]
     langs = scores.shape[1]
@@ -361,7 +388,7 @@
         own[s] = picked
 
     left, right = own[:, 0, :], own[:, 1, :]
-    logits_ref[...] = own[:, 2, :][:, :langs]
+    result_ref[:, :LANES] = own[:, 2, :]
     squares = jnp.sum(left * left + right * right, axis=1, keepdims=True)
     factor = lax.rsqrt(squares / width + EPS_NORM)
     mine = jnp.concatenate([left * factor, right * factor], axis=1).astype(BF16)
@@ -390,11 +417,15 @@
             device_id_type=MESH,
         ).wait_recv()
     every = gathered[...].reshape(members * stored, 2 * LANES).astype(BF16)
-    sim_ref[...] = (
-        lax.dot_general(mine, every, (((1,), (1,)), ((), ())), preferred_element_type=F32) / width
-    )
+    inner = lax.dot_general(mine, every, (((1,), (1,)), ((), ())), preferred_element_type=F32)
+    result_ref[:, LANES : LANES + members * stored] = inner / width
     for copy in sends:
         copy.wait_send()
+
+
+def split_result(result_ref, logits_ref, sim_ref):
+    logits_ref[0] = result_ref[:, : logits_ref.shape[2]]
+    sim_ref[0] = result_ref[:, LANES : LANES + sim_ref.shape[2]]
 
 
 def shards(
@@ -428,24 +459,22 @@
         excite_weight,
         attend_weight[0],
         score_weight[0],
-        embed_weight[0],
+        embed_weight[0].T,
         language_weight[0],
     )
     copied = [pltpu.VMEM(a.shape, a.dtype) for a in operands]
     del copied[1]
     copied[1] = pltpu.VMEM((WINDOW, channels), BF16)
+    copied[3] = pltpu.VMEM((SCALE - 1, 4 * LANES, 2 * LANES), BF16)
     anywhere = pl.BlockSpec(memory_space=pl.ANY)
     in_specs = [anywhere] * len(operands)
     in_specs[1] = pl.BlockSpec(memory_space=pltpu.SMEM)
     dma = pltpu.SemaphoreType.DMA
-    logits, similarity = pl.pallas_call(
+    result = pl.pallas_call(
         functools.partial(kernel, groups, members),
-        out_shape=(
-            jax.ShapeDtypeStruct((stored, langs), F32),
-            jax.ShapeDtypeStruct((stored, members * stored), F32),
-        ),
+        out_shape=jax.ShapeDtypeStruct((stored, 2 * LANES), F32),
         in_specs=in_specs,
-        out_specs=[pl.BlockSpec(memory_space=pltpu.VMEM)] * 2,
+        out_specs=pl.BlockSpec(memory_space=pltpu.VMEM),
         scratch_shapes=copied
         + [
             pltpu.VMEM((stored * SEND_ROWS, LANES), F32),
@@ -456,15 +485,15 @@
             pltpu.VMEM((rows, channels), BF16),
             pltpu.VMEM((rows, channels), BF16),
             pltpu.VMEM((rows, channels), F32),
-            pltpu.VMEM((rows + 4 * groups, LANES), BF16),
-            pltpu.VMEM((rows + 4 * groups, LANES), BF16),
+            pltpu.VMEM((2, rows // 2 + 2 * groups, LANES), BF16),
+            pltpu.VMEM((2, rows // 2 + 2 * groups, LANES), BF16),
             pltpu.VMEM((rows, LANES), F32),
             pltpu.VMEM((groups, 8, LANES), F32),
             pltpu.VMEM((groups, 8, LANES), F32),
             pltpu.VMEM((stored, 8, LANES), F32),
             pltpu.VMEM((stored, 2 * LANES), F32),
             pltpu.VMEM((members, stored, 2 * LANES), F32),
-            dma((len(copied),)),
+            dma((len(copied) + 1,)),
             dma((groups,)),
             dma((groups,)),
             dma((groups,)),
@@ -479,7 +508,13 @@
             flops=rows * 12_000_000, bytes_accessed=10_000_000, transcendentals=rows * 1200
         ),
     )(*operands)
-    return (logits[None], similarity[None])
+    return pl.pallas_call(
+        split_result,
+        out_shape=(
+            jax.ShapeDtypeStruct((1, stored, langs), F32),
+            jax.ShapeDtypeStruct((1, stored, members * stored), F32),
+        ),
+    )(result)
 
 
 def solution(mesh):

time: 48.5 us -> 42.2 us (0.87)
  local copies, waits for them, and re-layouts: 4.77 us -> 0 us
  Pallas kernels: 42.8 us -> 41.3 us
    unnamed x3 -> x0, local copies, waits for them, and re-layouts: 4.77 us -> none
    pallas_call x1 -> x2, Pallas kernels: 42.8 us -> 41.3 us  [the longest x1 40 us: shards(): pl.pallas_call(functools.partial(kernel, groups, members), out_shape=jax....]
where the time goes in v2:
time: 42.2 us; the launch traced here: 42 us
  Pallas kernels  41.3 us (98%)
  between operations  0.64 us (2%)
    pallas_call x1, Pallas kernels, shards(): pl.pallas_call(functools.partial(kernel, groups, members), out_shape=jax....  40 us
    pallas_call x1, Pallas kernels, shards(): pl.pallas_call(split_result, out_shape=(jax.ShapeDtypeStruct((1, stored,...  1.3 us

profile of v2, /device:TPU:0, one launch (start us, length us, event | category | flops | bytes accessed | tf_op | source)
XLA Modules:
  0.0 42.0 jit_solution(15742702902396954806)
XLA Ops:
  0.6 40.0 %shard_map.131.result_ref = f32[8,256]{1,0:T(8,128)} custom-call(f32[8,16000]{1,0:T(8,128)} %bitcast.9, s32[1,8]{1,0:T(1,128)} %dest_ref.1, bf16[400,1024]{1,0:T(8,128)(2,1)} %w0_hbm.1, bf16[1024,1024]{1,0:T(8,128)(2,1)} %expand_hbm.1, bf16[7,384,128]{2,1,0:T(8,128)(2,1)} %branch_hbm.1, bf16[1024,1024]{1,0:T(8,128)(2,1)} %merge_hbm.1, ...), custom_call_target="tpu_custom_call" | custom-call | flops 19200000000 | bytes 10000000 | tf_op jit(solution)/shard_map/pallas_call | solution.py:473
  40.7 1.3 %shard_map.132 = (f32[1,8,107]{2,1,0:T(8,128)}, f32[1,8,32]{2,1,0:T(8,128)}) custom-call(f32[8,256]{1,0:T(8,128)} %shard_map.131.result_ref), custom_call_target="tpu_custom_call" | custom-call | tf_op jit(solution)/shard_map/pallas_call | solution.py:511

commit v3 on v2

--- a/solution.py
+++ b/solution.py
@@ -18,6 +18,7 @@
 TAPS0 = 5
 WINDOW = 512
 TILE = 400
+TALL = 800
 CHUNK = 256
 EPS_STAT = 1e-05
 EPS_NORM = 1e-06
@@ -93,7 +94,7 @@
     stored = bank.shape[0]
     rows_all = FRAMES * groups
     tiles = rows_all // TILE
-    tile_frames = TILE // groups
+    talls = rows_all // TALL
     channels = front.shape[1]
     me = lax.axis_index("grp")
     my_mem = lax.axis_index("mem")
@@ -231,23 +232,24 @@
     loads[2].wait()
 
     chunks = [slice(c, c + CHUNK) for c in range(0, channels, CHUNK)]
-    half_tiles = tiles // 2
+    narrow = [slice(c, c + LANES) for c in range(0, channels, LANES)]
+    half_talls = talls // 2
 
     def first_layers(tile, _):
-        rows = pl.ds(pl.multiple_of(tile * TILE, 16), TILE)
+        rows = pl.ds(pl.multiple_of(tile * TALL, 16), TALL)
         for chunk in chunks:
             out = jnp.maximum(dot(cols[rows, :], w0[:, chunk]), 0.0)
             front[rows, chunk] = out.astype(BF16)
-        side = tile // half_tiles
-        start = pl.multiple_of(tile % half_tiles * TILE + side * halo, 16)
+        side = tile // half_talls
+        start = pl.multiple_of(tile % half_talls * TALL + side * halo, 16)
         for chunk in chunks:
             expanded = jnp.maximum(dot(front[rows, :], expand[:, chunk]), 0.0).astype(BF16)
             work[rows, chunk] = expanded
             if chunk.start == 0:
-                ping[side, pl.ds(start, TILE), :] = expanded[:, LANES : 2 * LANES]
+                ping[side, pl.ds(start, TALL), :] = expanded[:, LANES : 2 * LANES]
         return 0
 
-    lax.fori_loop(0, tiles, first_layers, 0)
+    lax.fori_loop(0, talls, first_layers, 0)
 
     loads[3].wait()
     loads[4].wait()
@@ -256,14 +258,14 @@
         source, target = buffers[(i - 1) % 2], buffers[i % 2]
 
         def one_branch(tile, _, i=i, source=source, target=target):
-            start = pl.multiple_of(tile * TILE, 16)
-            near, far = pl.ds(start, TILE), pl.ds(start + halo, TILE)
+            start = pl.multiple_of(tile * TALL, 16)
+            near, far = pl.ds(start, TALL), pl.ds(start + halo, TALL)
             window = jnp.concatenate(
                 [source[1, near, :], source[0, near, :], source[1, far, :], source[0, far, :]], axis=1
             )
             out = jnp.maximum(dot(window, branch[i - 1]), 0.0).astype(BF16)
             for side, spot in ((0, near), (1, far)):
-                rows = pl.ds(start + side * half, TILE)
+                rows = pl.ds(start + side * half, TALL)
                 mine = out[:, side * LANES : (side + 1) * LANES]
                 work[rows, i * LANES : (i + 1) * LANES] = mine
                 if i < SCALE - 1:
@@ -271,15 +273,15 @@
                     target[side, spot, :] = (following + mine.astype(F32)).astype(BF16)
             return 0
 
-        lax.fori_loop(0, half_tiles, one_branch, 0, unroll=True)
+        lax.fori_loop(0, half_talls, one_branch, 0, unroll=True)
 
     loads[5].wait()
 
     def by_frame(values):
-        return values.reshape(tile_frames, groups, values.shape[1])
+        return values.reshape(values.shape[0] // groups, groups, values.shape[1])
 
     def merging(tile, total):
-        rows = pl.ds(pl.multiple_of(tile * TILE, 16), TILE)
+        rows = pl.ds(pl.multiple_of(tile * TALL, 16), TALL)
         sums = []
         for chunk in chunks:
             merged = jnp.maximum(dot(work[rows, :], merge[:, chunk]), 0.0)
@@ -288,7 +290,7 @@
         return total + jnp.concatenate(sums, axis=1)
 
     zeros = jnp.zeros((groups, channels), F32)
-    total = lax.fori_loop(0, tiles, merging, zeros)
+    total = lax.fori_loop(0, talls, merging, zeros)
 
     loads[6].wait()
     loads[7].wait()
@@ -302,12 +304,11 @@
         first, second = carry
         rows = pl.ds(pl.multiple_of(tile * TILE, 16), TILE)
         sums, squares = [], []
-        for chunk in chunks:
+        for chunk in narrow:
             out = by_frame(wide[rows, chunk]) * excited[:, chunk]
             out = by_frame(front[rows, chunk].astype(F32)) + out
-            out = out.reshape(TILE, CHUNK).astype(BF16)
-            work[rows, chunk] = out
-            moved = by_frame(out.astype(F32)) - pivot[:, chunk]
+            work[rows, chunk] = out.reshape(TILE, LANES).astype(BF16)
+            moved = out - pivot[:, chunk]
             sums.append(jnp.sum(moved, axis=0))
             squares.append(jnp.sum(moved * moved, axis=0))
         attn[rows, :] = dot(work[rows, :], attend[0:channels, :])

time: 42.2 us -> 42.4 us (level)
  no operation moved by 1% of the time
where the time goes in v3:
time: 42.4 us; the launch traced here: 42.2 us
  Pallas kernels  41.6 us (98%)
  between operations  0.64 us (2%)
    pallas_call x1, Pallas kernels, shards(): pl.pallas_call(functools.partial(kernel, groups, members), out_shape=jax....  40.3 us
    pallas_call x1, Pallas kernels, shards(): pl.pallas_call(split_result, out_shape=(jax.ShapeDtypeStruct((1, stored,...  1.3 us

profile of v3, /device:TPU:0, one launch (start us, length us, event | category | flops | bytes accessed | tf_op | source)
XLA Modules:
  0.0 42.2 jit_solution(6050361577556313815)
XLA Ops:
  0.6 40.3 %shard_map.131.result_ref = f32[8,256]{1,0:T(8,128)} custom-call(f32[8,16000]{1,0:T(8,128)} %bitcast.9, s32[1,8]{1,0:T(1,128)} %dest_ref.1, bf16[400,1024]{1,0:T(8,128)(2,1)} %w0_hbm.1, bf16[1024,1024]{1,0:T(8,128)(2,1)} %expand_hbm.1, bf16[7,384,128]{2,1,0:T(8,128)(2,1)} %branch_hbm.1, bf16[1024,1024]{1,0:T(8,128)(2,1)} %merge_hbm.1, ...), custom_call_target="tpu_custom_call" | custom-call | flops 19200000000 | bytes 10000000 | tf_op jit(solution)/shard_map/pallas_call | solution.py:474
  40.9 1.3 %shard_map.132 = (f32[1,8,107]{2,1,0:T(8,128)}, f32[1,8,32]{2,1,0:T(8,128)}) custom-call(f32[8,256]{1,0:T(8,128)} %shard_map.131.result_ref), custom_call_target="tpu_custom_call" | custom-call | tf_op jit(solution)/shard_map/pallas_call | solution.py:512

commit v4 on v2

--- a/solution.py
+++ b/solution.py
@@ -12,6 +12,8 @@
 FRAMES = 200
 LANES = 128
 FLAT_ROWS = 125
+TAG_ROW = 127
+PART_ROWS = 64
 SEND_ROWS = 128
 LEAD = 8
 SLOT_ROWS = LEAD + SEND_ROWS
@@ -80,20 +82,15 @@
     back,
     home,
     own,
-    normed,
-    gathered,
     load_sem,
     out_send,
     out_recv,
     back_send,
     back_recv,
-    mem_send,
-    mem_recv,
 ):
     stored = bank.shape[0]
     rows_all = FRAMES * groups
     tiles = rows_all // TILE
-    tile_frames = TILE // groups
     channels = front.shape[1]
     me = lax.axis_index("grp")
     my_mem = lax.axis_index("mem")
@@ -120,14 +117,13 @@
         load.start()
 
     barrier = pltpu.get_barrier_semaphore()
-    for step in range(1, groups):
-        pl.semaphore_signal(
-            barrier, inc=1, device_id=(lax.rem(me + step, groups), my_mem), device_id_type=MESH
-        )
-    for step in range(1, members):
-        pl.semaphore_signal(
-            barrier, inc=1, device_id=(me, lax.rem(my_mem + step, members)), device_id_type=MESH
-        )
+    others = [(g, m) for m in range(members) for g in range(groups) if g or m]
+
+    def other(group_step, member_step):
+        return (lax.rem(me + group_step, groups), lax.rem(my_mem + member_step, members))
+
+    for steps in others:
+        pl.semaphore_signal(barrier, inc=1, device_id=other(*steps), device_id_type=MESH)
 
     staged[...] = jnp.zeros_like(staged)
     slots[...] = jnp.zeros_like(slots)
@@ -142,57 +138,71 @@
     branch[:, :LANES, LANES:] = empty
     back[...] = jnp.zeros_like(back)
 
-    loads[0].wait()
-    for row in range(FLAT_ROWS):
-        staged[pl.ds(row, stored, stride=SEND_ROWS), :] = bank[:, row * LANES : (row + 1) * LANES]
-
-    def segment_for(group):
-        picked = jnp.zeros((SEND_ROWS, LANES), F32)
+    for s in range(stored):
+        staged[s * SEND_ROWS + TAG_ROW : s * SEND_ROWS + TAG_ROW + 1, :] = jnp.full(
+            (1, LANES), s + 1, F32
+        )
+
+    def stage(first, last):
+        for row in range(first, last):
+            staged[pl.ds(row, stored, stride=SEND_ROWS), :] = bank[
+                :, row * LANES : (row + 1) * LANES
+            ]
+
+    def part_for(group, part):
+        picked = jnp.zeros((PART_ROWS, LANES), F32)
         for s in range(stored):
-            rows = staged[s * SEND_ROWS : (s + 1) * SEND_ROWS, :]
+            first = s * SEND_ROWS + part * PART_ROWS
+            rows = staged[first : first + PART_ROWS, :]
             picked = jnp.where(dest_ref[0, s] == group, rows, picked)
         return picked.astype(BF16)
 
-    for step in range(1, groups):
-        outbox[step] = segment_for(lax.rem(me + step, groups))
-
-    pl.semaphore_wait(barrier, groups - 1 + members - 1)
-
-    sends = []
-    for step in range(1, groups):
-        group = lax.rem(me + step, groups)
-        copy = pltpu.make_async_remote_copy(
-            src_ref=outbox.at[step],
-            dst_ref=arrived.at[me],
-            send_sem=out_send.at[step],
-            recv_sem=out_recv.at[me],
+    def fill(part):
+        for step in range(1, groups):
+            outbox[part, step] = part_for(lax.rem(me + step, groups), part)
+        arrived[part, me] = part_for(me, part)
+
+    def routed(part, step, source, group):
+        return pltpu.make_async_remote_copy(
+            src_ref=outbox.at[part, step],
+            dst_ref=arrived.at[part, source],
+            send_sem=out_send.at[part, step],
+            recv_sem=out_recv.at[part, source],
             device_id=(group, my_mem),
             device_id_type=MESH,
         )
-        copy.start()
-        sends.append(copy)
-    arrived[me] = segment_for(me)
-
-    def place(slot):
-        start = pl.multiple_of(slot * SLOT_ROWS + LEAD, 8)
-        slots[pl.ds(start, SEND_ROWS), :] = arrived[slot].astype(F32)
-
-    place(me)
-    for step in range(1, groups):
-        source = lax.rem(me + groups - step, groups)
-        pltpu.make_async_remote_copy(
-            src_ref=outbox.at[step],
-            dst_ref=arrived.at[source],
-            send_sem=out_send.at[step],
-            recv_sem=out_recv.at[source],
-            device_id=(source, my_mem),
-            device_id_type=MESH,
-        ).wait_recv()
-        place(source)
+
+    sends = []
+
+    def send(part):
+        for step in range(1, groups):
+            copy = routed(part, step, me, lax.rem(me + step, groups))
+            copy.start()
+            sends.append(copy)
+
+    def place(part, slot):
+        start = pl.multiple_of(slot * SLOT_ROWS + LEAD + part * PART_ROWS, 8)
+        slots[pl.ds(start, PART_ROWS), :] = arrived[part, slot].astype(F32)
+
+    def receive(part):
+        place(part, me)
+        for step in range(1, groups):
+            source = lax.rem(me + groups - step, groups)
+            routed(part, step, source, source).wait_recv()
+            place(part, source)
+
+    loads[0].wait()
+    stage(0, PART_ROWS)
+    fill(0)
+    pl.semaphore_wait(barrier, len(others))
+    send(0)
+    stage(PART_ROWS, FLAT_ROWS)
+    fill(1)
+    send(1)
 
     lane = lax.broadcasted_iota(jnp.int32, (groups, LANES), 1)
 
-    def windows(block, _):
+    def windows(block, _, phases=range(8)):
         first = block * 5
         held = {}
 
@@ -202,7 +212,7 @@
             return held[index]
 
         pair = []
-        for phase in range(8):
+        for phase in phases:
             begin = phase * MELS + LEAD * LANES - 2 * MELS
             index, offset = begin // LANES, begin % LANES
             pieces = []
@@ -225,29 +235,41 @@
                 pair = []
         return 0
 
-    lax.fori_loop(0, FRAMES // 8, windows, 0)
-
-    loads[1].wait()
-    loads[2].wait()
 
     chunks = [slice(c, c + CHUNK) for c in range(0, channels, CHUNK)]
+    narrow = [slice(c, c + LANES) for c in range(0, channels, LANES)]
     half_tiles = tiles // 2
-
-    def first_layers(tile, _):
+    part_tiles = half_tiles // 2
+
+    def first_layers(step, _, part):
+        side = step // part_tiles
+        start = side * half_tiles + part * part_tiles + step % part_tiles
+        rows_of_tile(side, start)
+        return 0
+
+    def rows_of_tile(side, tile):
         rows = pl.ds(pl.multiple_of(tile * TILE, 16), TILE)
         for chunk in chunks:
             out = jnp.maximum(dot(cols[rows, :], w0[:, chunk]), 0.0)
             front[rows, chunk] = out.astype(BF16)
-        side = tile // half_tiles
         start = pl.multiple_of(tile % half_tiles * TILE + side * halo, 16)
         for chunk in chunks:
             expanded = jnp.maximum(dot(front[rows, :], expand[:, chunk]), 0.0).astype(BF16)
             work[rows, chunk] = expanded
             if chunk.start == 0:
                 ping[side, pl.ds(start, TILE), :] = expanded[:, LANES : 2 * LANES]
-        return 0
-
-    lax.fori_loop(0, tiles, first_layers, 0)
+
+    split = FRAMES // 16
+    receive(0)
+    lax.fori_loop(0, split, windows, 0)
+    windows(split, 0, range(4))
+    loads[1].wait()
+    loads[2].wait()
+    lax.fori_loop(0, half_tiles, functools.partial(first_layers, part=0), 0)
+    receive(1)
+    windows(split, 0, range(4, 8))
+    lax.fori_loop(split + 1, FRAMES // 8, windows, 0)
+    lax.fori_loop(0, half_tiles, functools.partial(first_layers, part=1), 0)
 
     loads[3].wait()
     loads[4].wait()
@@ -276,7 +298,7 @@
     loads[5].wait()
 
     def by_frame(values):
-        return values.reshape(tile_frames, groups, values.shape[1])
+        return values.reshape(values.shape[0] // groups, groups, values.shape[1])
 
     def merging(tile, total):
         rows = pl.ds(pl.multiple_of(tile * TILE, 16), TILE)
@@ -302,12 +324,11 @@
         first, second = carry
         rows = pl.ds(pl.multiple_of(tile * TILE, 16), TILE)
         sums, squares = [], []
-        for chunk in chunks:
+        for chunk in narrow:
             out = by_frame(wide[rows, chunk]) * excited[:, chunk]
             out = by_frame(front[rows, chunk].astype(F32)) + out
-            out = out.reshape(TILE, CHUNK).astype(BF16)
-            work[rows, chunk] = out
-            moved = by_frame(out.astype(F32)) - pivot[:, chunk]
+            work[rows, chunk] = out.reshape(TILE, LANES).astype(BF16)
+            moved = out - pivot[:, chunk]
             sums.append(jnp.sum(moved, axis=0))
             squares.append(jnp.sum(moved * moved, axis=0))
         attn[rows, :] = dot(work[rows, :], attend[0:channels, :])
@@ -354,71 +375,53 @@
     scores = dot(embedding.astype(BF16), lang[...])
     width = embedding.shape[1]
     langs = scores.shape[1]
-    back[:, 0, :] = embedding[:, :LANES]
-    back[:, 1, : width - LANES] = embedding[:, LANES:]
+    squares = jnp.sum(embedding * embedding, axis=1, keepdims=True)
+    factor = lax.rsqrt(squares / width + EPS_NORM)
+    normed = (embedding * factor).astype(BF16).astype(F32)
+    back[:, 0, :] = normed[:, :LANES]
+    back[:, 1, : width - LANES] = normed[:, LANES:]
     back[:, 2, :langs] = scores
-
-    for step in range(1, groups):
-        group = lax.rem(me + step, groups)
-        copy = pltpu.make_async_remote_copy(
-            src_ref=back.at[group],
-            dst_ref=home.at[me],
-            send_sem=back_send.at[step],
-            recv_sem=back_recv.at[me],
-            device_id=(group, my_mem),
+    back[:, 3, :] = slots[pl.ds(LEAD + TAG_ROW, groups, stride=SLOT_ROWS), :]
+
+    def returned(group_step, member_step, source, target):
+        return pltpu.make_async_remote_copy(
+            src_ref=back.at[target[0]],
+            dst_ref=home.at[source[1], source[0]],
+            send_sem=back_send.at[member_step, group_step],
+            recv_sem=back_recv.at[source[1], source[0]],
+            device_id=target,
             device_id_type=MESH,
         )
+
+    for steps in others:
+        copy = returned(*steps, (me, my_mem), other(*steps))
         copy.start()
         sends.append(copy)
-    home[me] = back[me]
-    for step in range(1, groups):
-        source = lax.rem(me + groups - step, groups)
-        pltpu.make_async_remote_copy(
-            src_ref=back.at[source],
-            dst_ref=home.at[source],
-            send_sem=back_send.at[step],
-            recv_sem=back_recv.at[source],
-            device_id=(source, my_mem),
-            device_id_type=MESH,
-        ).wait_recv()
+    home[my_mem, me] = back[me]
+    for group_step, member_step in others:
+        source = (
+            lax.rem(me + groups - group_step, groups),
+            lax.rem(my_mem + members - member_step, members),
+        )
+        returned(group_step, member_step, source, source).wait_recv()
+
     for s in range(stored):
-        picked = home[0]
+        picked = home[my_mem, 0]
         for group in range(1, groups):
-            picked = jnp.where(dest_ref[0, s] == group, home[group], picked)
+            picked = jnp.where(dest_ref[0, s] == group, home[my_mem, group], picked)
         own[s] = picked
-
-    left, right = own[:, 0, :], own[:, 1, :]
     result_ref[:, :LANES] = own[:, 2, :]
-    squares = jnp.sum(left * left + right * right, axis=1, keepdims=True)
-    factor = lax.rsqrt(squares / width + EPS_NORM)
-    mine = jnp.concatenate([left * factor, right * factor], axis=1).astype(BF16)
-    normed[...] = mine.astype(F32)
-    for step in range(1, members):
-        member = lax.rem(my_mem + step, members)
-        copy = pltpu.make_async_remote_copy(
-            src_ref=normed,
-            dst_ref=gathered.at[my_mem],
-            send_sem=mem_send.at[step],
-            recv_sem=mem_recv.at[my_mem],
-            device_id=(me, member),
-            device_id_type=MESH,
-        )
-        copy.start()
-        sends.append(copy)
-    gathered[my_mem] = normed[...]
-    for step in range(1, members):
-        source = lax.rem(my_mem + members - step, members)
-        pltpu.make_async_remote_copy(
-            src_ref=normed,
-            dst_ref=gathered.at[source],
-            send_sem=mem_send.at[step],
-            recv_sem=mem_recv.at[source],
-            device_id=(me, source),
-            device_id_type=MESH,
-        ).wait_recv()
-    every = gathered[...].reshape(members * stored, 2 * LANES).astype(BF16)
-    inner = lax.dot_general(mine, every, (((1,), (1,)), ((), ())), preferred_element_type=F32)
-    result_ref[:, LANES : LANES + members * stored] = inner / width
+    mine = jnp.concatenate([own[:, 0, :], own[:, 1, :]], axis=1).astype(BF16)
+    count = members * groups
+    every = home[...].reshape(count, 8, LANES)
+    placed = jnp.concatenate([every[:, 0, :], every[:, 1, :]], axis=1).astype(BF16)
+    inner = lax.dot_general(mine, placed, (((1,), (1,)), ((), ())), preferred_element_type=F32)
+    slot = lax.broadcasted_iota(jnp.int32, (count, LANES), 0)
+    column = lax.broadcasted_iota(jnp.int32, (count, LANES), 1)
+    tags = every[:, 3, :]
+    wanted = (column - slot // groups * stored + 1).astype(F32)
+    chosen = jnp.where((tags > 0.0) & (tags == wanted), 1.0, 0.0).astype(BF16)
+    result_ref[:, LANES:] = dot_split(inner / width, chosen)
     for copy in sends:
         copy.wait_send()
 
@@ -478,8 +481,8 @@
         scratch_shapes=copied
         + [
             pltpu.VMEM((stored * SEND_ROWS, LANES), F32),
-            pltpu.VMEM((groups, SEND_ROWS, LANES), BF16),
-            pltpu.VMEM((groups, SEND_ROWS, LANES), BF16),
+            pltpu.VMEM((2, groups, PART_ROWS, LANES), BF16),
+            pltpu.VMEM((2, groups, PART_ROWS, LANES), BF16),
             pltpu.VMEM((groups * SLOT_ROWS, LANES), F32),
             pltpu.VMEM((rows, WINDOW), BF16),
             pltpu.VMEM((rows, channels), BF16),
@@ -489,17 +492,13 @@
             pltpu.VMEM((2, rows // 2 + 2 * groups, LANES), BF16),
             pltpu.VMEM((rows, LANES), F32),
             pltpu.VMEM((groups, 8, LANES), F32),
-            pltpu.VMEM((groups, 8, LANES), F32),
+            pltpu.VMEM((members, groups, 8, LANES), F32),
             pltpu.VMEM((stored, 8, LANES), F32),
-            pltpu.VMEM((stored, 2 * LANES), F32),
-            pltpu.VMEM((members, stored, 2 * LANES), F32),
             dma((len(copied) + 1,)),
-            dma((groups,)),
-            dma((groups,)),
-            dma((groups,)),
-            dma((groups,)),
-            dma((members,)),
-            dma((members,)),
+            dma((2, groups)),
+            dma((2, groups)),
+            dma((members, groups)),
+            dma((members, groups)),
         ],
         compiler_params=pltpu.CompilerParams(
             collective_id=0, has_side_effects=True, vmem_limit_bytes=60 * 1024 * 1024

time: 42.2 us -> 41.7 us (0.988)
  Pallas kernels: 41.3 us -> 40.8 us
    pallas_call x1, Pallas kernels: 40 us -> 39.5 us  [shards(): pl.pallas_call(functools.partial(kernel, groups, members), out_shape=jax....]
where the time goes in v4:
time: 41.7 us; the launch traced here: 41.5 us
  Pallas kernels  40.8 us (98%)
  between operations  0.64 us (2%)
    pallas_call x1, Pallas kernels, shards(): pl.pallas_call(functools.partial(kernel, groups, members), out_shape=jax....  39.5 us
    pallas_call x1, Pallas kernels, shards(): pl.pallas_call(split_result, out_shape=(jax.ShapeDtypeStruct((1, stored,...  1.3 us

profile of v4, /device:TPU:0, one launch (start us, length us, event | category | flops | bytes accessed | tf_op | source)
XLA Modules:
  0.0 41.5 jit_solution(7906470155874242187)
XLA Ops:
  0.6 39.5 %shard_map.131.result_ref = f32[8,256]{1,0:T(8,128)} custom-call(f32[8,16000]{1,0:T(8,128)} %bitcast.9, s32[1,8]{1,0:T(1,128)} %dest_ref.1, bf16[400,1024]{1,0:T(8,128)(2,1)} %w0_hbm.1, bf16[1024,1024]{1,0:T(8,128)(2,1)} %expand_hbm.1, bf16[7,384,128]{2,1,0:T(8,128)(2,1)} %branch_hbm.1, bf16[1024,1024]{1,0:T(8,128)(2,1)} %merge_hbm.1, ...), custom_call_target="tpu_custom_call" | custom-call | flops 19200000000 | bytes 10000000 | tf_op jit(solution)/shard_map/pallas_call | solution.py:476
  40.2 1.3 %shard_map.132 = (f32[1,8,107]{2,1,0:T(8,128)}, f32[1,8,32]{2,1,0:T(8,128)}) custom-call(f32[8,256]{1,0:T(8,128)} %shard_map.131.result_ref), custom_call_target="tpu_custom_call" | custom-call | tf_op jit(solution)/shard_map/pallas_call | solution.py:510

commit v5 on v4

--- a/solution.py
+++ b/solution.py
@@ -21,6 +21,8 @@
 WINDOW = 512
 TILE = 400
 CHUNK = 256
+SHORT = 160
+PIECE = 16
 EPS_STAT = 1e-05
 EPS_NORM = 1e-06
 
@@ -301,12 +303,19 @@
         return values.reshape(values.shape[0] // groups, groups, values.shape[1])
 
     def merging(tile, total):
-        rows = pl.ds(pl.multiple_of(tile * TILE, 16), TILE)
+        start = pl.multiple_of(tile * TILE, 16)
+        rows = pl.ds(start, TILE)
         sums = []
         for chunk in chunks:
-            merged = jnp.maximum(dot(work[rows, :], merge[:, chunk]), 0.0)
-            wide[rows, chunk] = merged
-            sums.append(jnp.sum(by_frame(merged), axis=0))
+            product = dot(work[rows, :], merge[:, chunk])
+            for lanes in range(0, CHUNK, LANES):
+                column = slice(chunk.start + lanes, chunk.start + lanes + LANES)
+                part = jnp.zeros((groups, LANES), F32)
+                for piece in range(0, TILE, PIECE):
+                    merged = jnp.maximum(product[piece : piece + PIECE, lanes : lanes + LANES], 0.0)
+                    wide[pl.ds(start + piece, PIECE), column] = merged
+                    part = part + jnp.sum(by_frame(merged), axis=0)
+                sums.append(part)
         return total + jnp.concatenate(sums, axis=1)
 
     zeros = jnp.zeros((groups, channels), F32)
@@ -322,19 +331,26 @@
 
     def trunk_out(tile, carry):
         first, second = carry
-        rows = pl.ds(pl.multiple_of(tile * TILE, 16), TILE)
+        start = pl.multiple_of(tile * SHORT, 16)
         sums, squares = [], []
-        for chunk in narrow:
-            out = by_frame(wide[rows, chunk]) * excited[:, chunk]
-            out = by_frame(front[rows, chunk].astype(F32)) + out
-            work[rows, chunk] = out.reshape(TILE, LANES).astype(BF16)
-            moved = out - pivot[:, chunk]
-            sums.append(jnp.sum(moved, axis=0))
-            squares.append(jnp.sum(moved * moved, axis=0))
+        for column in narrow:
+            gain, middle = excited[:, column], pivot[:, column]
+            part = jnp.zeros((groups, LANES), F32)
+            square = part
+            for piece in range(0, SHORT, PIECE):
+                rows = pl.ds(start + piece, PIECE)
+                out = by_frame(front[rows, column].astype(F32)) + by_frame(wide[rows, column]) * gain
+                work[rows, column] = out.reshape(PIECE, LANES).astype(BF16)
+                moved = out - middle
+                part = part + jnp.sum(moved, axis=0)
+                square = square + jnp.sum(moved * moved, axis=0)
+            sums.append(part)
+            squares.append(square)
+        rows = pl.ds(start, SHORT)
         attn[rows, :] = dot(work[rows, :], attend[0:channels, :])
         return first + jnp.concatenate(sums, axis=1), second + jnp.concatenate(squares, axis=1)
 
-    first, second = lax.fori_loop(0, tiles, trunk_out, (zeros, zeros))
+    first, second = lax.fori_loop(0, rows_all // SHORT, trunk_out, (zeros, zeros))
     shift = first / FRAMES
     center = pivot + shift
     spread = jnp.sqrt(jnp.maximum(second / FRAMES - shift * shift, 0.0) + EPS_STAT)
@@ -347,20 +363,30 @@
     inverse = 1.0 / spread
 
     def energies(tile, carry):
-        rows = pl.ds(pl.multiple_of(tile * TILE, 16), TILE)
-        attended = jnp.tanh(by_frame(attn[rows, :]) + context).reshape(TILE, -1).astype(BF16)
+        start = pl.multiple_of(tile * SHORT, 16)
+        rows = pl.ds(start, SHORT)
+        attended = jnp.tanh(by_frame(attn[rows, :]) + context).reshape(SHORT, LANES).astype(BF16)
         parts = ([], [], [])
         for chunk in chunks:
-            weights = by_frame(jnp.exp(dot(attended, score[:, chunk])))
-            value = by_frame(work[rows, chunk].astype(F32))
-            value = (value - center[:, chunk]) * inverse[:, chunk]
-            parts[0].append(jnp.sum(weights, axis=0))
-            weights = weights * value
-            parts[1].append(jnp.sum(weights, axis=0))
-            parts[2].append(jnp.sum(weights * value, axis=0))
+            product = dot(attended, score[:, chunk])
+            for lanes in range(0, CHUNK, LANES):
+                column = slice(chunk.start + lanes, chunk.start + lanes + LANES)
+                middle, gain = center[:, column], inverse[:, column]
+                sums = [jnp.zeros((groups, LANES), F32)] * 3
+                for piece in range(0, SHORT, PIECE):
+                    weights = by_frame(
+                        jnp.exp(product[piece : piece + PIECE, lanes : lanes + LANES])
+                    )
+                    value = by_frame(work[pl.ds(start + piece, PIECE), column].astype(F32))
+                    value = (value - middle) * gain
+                    once = weights * value
+                    for k, term in enumerate((weights, once, once * value)):
+                        sums[k] = sums[k] + jnp.sum(term, axis=0)
+                for k in range(3):
+                    parts[k].append(sums[k])
         return tuple(c + jnp.concatenate(p, axis=1) for c, p in zip(carry, parts))
 
-    norm, weighted, squared = lax.fori_loop(0, tiles, energies, (zeros, zeros, zeros))
+    norm, weighted, squared = lax.fori_loop(0, rows_all // SHORT, energies, (zeros, zeros, zeros))
     weighted = weighted / norm
     squared = jnp.maximum(squared / norm - weighted * weighted, 0.0)
     mean = center + spread * weighted

time: 41.7 us -> 44.1 us (1.058)
  Pallas kernels: 40.8 us -> 43.2 us
    pallas_call x1, Pallas kernels: 39.5 us -> 41.9 us  [shards(): pl.pallas_call(functools.partial(kernel, groups, members), out_shape=jax....]
where the time goes in v5:
time: 44.1 us; the launch traced here: 43.9 us
  Pallas kernels  43.2 us (98%)
  between operations  0.64 us (1%)
    pallas_call x1, Pallas kernels, shards(): pl.pallas_call(functools.partial(kernel, groups, members), out_shape=jax....  41.9 us
    pallas_call x1, Pallas kernels, shards(): pl.pallas_call(split_result, out_shape=(jax.ShapeDtypeStruct((1, stored,...  1.3 us

profile of v5, /device:TPU:0, one launch (start us, length us, event | category | flops | bytes accessed | tf_op | source)
XLA Modules:
  0.0 43.9 jit_solution(8133326629828745323)
XLA Ops:
  0.6 41.9 %shard_map.131.result_ref = f32[8,256]{1,0:T(8,128)} custom-call(f32[8,16000]{1,0:T(8,128)} %bitcast.9, s32[1,8]{1,0:T(1,128)} %dest_ref.1, bf16[400,1024]{1,0:T(8,128)(2,1)} %w0_hbm.1, bf16[1024,1024]{1,0:T(8,128)(2,1)} %expand_hbm.1, bf16[7,384,128]{2,1,0:T(8,128)(2,1)} %branch_hbm.1, bf16[1024,1024]{1,0:T(8,128)(2,1)} %merge_hbm.1, ...), custom_call_target="tpu_custom_call" | custom-call | flops 19200000000 | bytes 10000000 | tf_op jit(solution)/shard_map/pallas_call | solution.py:502
  42.6 1.3 %shard_map.132 = (f32[1,8,107]{2,1,0:T(8,128)}, f32[1,8,32]{2,1,0:T(8,128)}) custom-call(f32[8,256]{1,0:T(8,128)} %shard_map.131.result_ref), custom_call_target="tpu_custom_call" | custom-call | tf_op jit(solution)/shard_map/pallas_call | solution.py:536

commit v6 on v2

--- a/solution.py
+++ b/solution.py
@@ -12,6 +12,7 @@
 FRAMES = 200
 LANES = 128
 FLAT_ROWS = 125
+PART_ROWS = 64
 SEND_ROWS = 128
 LEAD = 8
 SLOT_ROWS = LEAD + SEND_ROWS
@@ -93,7 +94,6 @@
     stored = bank.shape[0]
     rows_all = FRAMES * groups
     tiles = rows_all // TILE
-    tile_frames = TILE // groups
     channels = front.shape[1]
     me = lax.axis_index("grp")
     my_mem = lax.axis_index("mem")
@@ -116,8 +116,7 @@
         pltpu.make_async_copy(source, target, load_sem.at[i])
         for i, (source, target) in enumerate(pairs)
     ]
-    for load in loads:
-        load.start()
+    loads[0].start()
 
     barrier = pltpu.get_barrier_semaphore()
     for step in range(1, groups):
@@ -130,6 +129,66 @@
         )
 
     staged[...] = jnp.zeros_like(staged)
+
+    def stage(first, last):
+        for row in range(first, last):
+            staged[pl.ds(row, stored, stride=SEND_ROWS), :] = bank[
+                :, row * LANES : (row + 1) * LANES
+            ]
+
+    def part_for(group, part):
+        picked = jnp.zeros((PART_ROWS, LANES), F32)
+        for s in range(stored):
+            first = s * SEND_ROWS + part * PART_ROWS
+            rows = staged[first : first + PART_ROWS, :]
+            picked = jnp.where(dest_ref[0, s] == group, rows, picked)
+        return picked.astype(BF16)
+
+    def fill(part):
+        for step in range(1, groups):
+            outbox[part, step] = part_for(lax.rem(me + step, groups), part)
+        arrived[part, me] = part_for(me, part)
+
+    def routed(part, step, source, group):
+        return pltpu.make_async_remote_copy(
+            src_ref=outbox.at[part, step],
+            dst_ref=arrived.at[part, source],
+            send_sem=out_send.at[part, step],
+            recv_sem=out_recv.at[part, source],
+            device_id=(group, my_mem),
+            device_id_type=MESH,
+        )
+
+    sends = []
+
+    def send(part):
+        for step in range(1, groups):
+            copy = routed(part, step, me, lax.rem(me + step, groups))
+            copy.start()
+            sends.append(copy)
+
+    def place(part, slot):
+        start = pl.multiple_of(slot * SLOT_ROWS + LEAD + part * PART_ROWS, 8)
+        slots[pl.ds(start, PART_ROWS), :] = arrived[part, slot].astype(F32)
+
+    def receive(part):
+        place(part, me)
+        for step in range(1, groups):
+            source = lax.rem(me + groups - step, groups)
+            routed(part, step, source, source).wait_recv()
+            place(part, source)
+
+    loads[0].wait()
+    stage(0, PART_ROWS)
+    fill(0)
+    pl.semaphore_wait(barrier, groups - 1 + members - 1)
+    send(0)
+    stage(PART_ROWS, FLAT_ROWS)
+    fill(1)
+    send(1)
+    for load in loads[1:]:
+        load.start()
+
     slots[...] = jnp.zeros_like(slots)
     w0[w0_hbm.shape[0] :, :] = jnp.zeros((WINDOW - w0_hbm.shape[0], channels), BF16)
     halo = 2 * groups
@@ -142,57 +201,9 @@
     branch[:, :LANES, LANES:] = empty
     back[...] = jnp.zeros_like(back)
 
-    loads[0].wait()
-    for row in range(FLAT_ROWS):
-        staged[pl.ds(row, stored, stride=SEND_ROWS), :] = bank[:, row * LANES : (row + 1) * LANES]
-
-    def segment_for(group):
-        picked = jnp.zeros((SEND_ROWS, LANES), F32)
-        for s in range(stored):
-            rows = staged[s * SEND_ROWS : (s + 1) * SEND_ROWS, :]
-            picked = jnp.where(dest_ref[0, s] == group, rows, picked)
-        return picked.astype(BF16)
-
-    for step in range(1, groups):
-        outbox[step] = segment_for(lax.rem(me + step, groups))
-
-    pl.semaphore_wait(barrier, groups - 1 + members - 1)
-
-    sends = []
-    for step in range(1, groups):
-        group = lax.rem(me + step, groups)
-        copy = pltpu.make_async_remote_copy(
-            src_ref=outbox.at[step],
-            dst_ref=arrived.at[me],
-            send_sem=out_send.at[step],
-            recv_sem=out_recv.at[me],
-            device_id=(group, my_mem),
-            device_id_type=MESH,
-        )
-        copy.start()
-        sends.append(copy)
-    arrived[me] = segment_for(me)
-
-    def place(slot):
-        start = pl.multiple_of(slot * SLOT_ROWS + LEAD, 8)
-        slots[pl.ds(start, SEND_ROWS), :] = arrived[slot].astype(F32)
-
-    place(me)
-    for step in range(1, groups):
-        source = lax.rem(me + groups - step, groups)
-        pltpu.make_async_remote_copy(
-            src_ref=outbox.at[step],
-            dst_ref=arrived.at[source],
-            send_sem=out_send.at[step],
-            recv_sem=out_recv.at[source],
-            device_id=(source, my_mem),
-            device_id_type=MESH,
-        ).wait_recv()
-        place(source)
-
     lane = lax.broadcasted_iota(jnp.int32, (groups, LANES), 1)
 
-    def windows(block, _):
+    def windows(block, _, phases=range(8)):
         first = block * 5
         held = {}
 
@@ -202,7 +213,7 @@
             return held[index]
 
         pair = []
-        for phase in range(8):
+        for phase in phases:
             begin = phase * MELS + LEAD * LANES - 2 * MELS
             index, offset = begin // LANES, begin % LANES
             pieces = []
@@ -225,29 +236,41 @@
                 pair = []
         return 0
 
-    lax.fori_loop(0, FRAMES // 8, windows, 0)
-
-    loads[1].wait()
-    loads[2].wait()
 
     chunks = [slice(c, c + CHUNK) for c in range(0, channels, CHUNK)]
+    narrow = [slice(c, c + LANES) for c in range(0, channels, LANES)]
     half_tiles = tiles // 2
-
-    def first_layers(tile, _):
+    part_tiles = half_tiles // 2
+
+    def first_layers(step, _, part):
+        side = step // part_tiles
+        start = side * half_tiles + part * part_tiles + step % part_tiles
+        rows_of_tile(side, start)
+        return 0
+
+    def rows_of_tile(side, tile):
         rows = pl.ds(pl.multiple_of(tile * TILE, 16), TILE)
         for chunk in chunks:
             out = jnp.maximum(dot(cols[rows, :], w0[:, chunk]), 0.0)
             front[rows, chunk] = out.astype(BF16)
-        side = tile // half_tiles
         start = pl.multiple_of(tile % half_tiles * TILE + side * halo, 16)
         for chunk in chunks:
             expanded = jnp.maximum(dot(front[rows, :], expand[:, chunk]), 0.0).astype(BF16)
             work[rows, chunk] = expanded
             if chunk.start == 0:
                 ping[side, pl.ds(start, TILE), :] = expanded[:, LANES : 2 * LANES]
-        return 0
-
-    lax.fori_loop(0, tiles, first_layers, 0)
+
+    split = FRAMES // 16
+    receive(0)
+    lax.fori_loop(0, split, windows, 0)
+    windows(split, 0, range(4))
+    loads[1].wait()
+    loads[2].wait()
+    lax.fori_loop(0, half_tiles, functools.partial(first_layers, part=0), 0)
+    receive(1)
+    windows(split, 0, range(4, 8))
+    lax.fori_loop(split + 1, FRAMES // 8, windows, 0)
+    lax.fori_loop(0, half_tiles, functools.partial(first_layers, part=1), 0)
 
     loads[3].wait()
     loads[4].wait()
@@ -276,7 +299,7 @@
     loads[5].wait()
 
     def by_frame(values):
-        return values.reshape(tile_frames, groups, values.shape[1])
+        return values.reshape(values.shape[0] // groups, groups, values.shape[1])
 
     def merging(tile, total):
         rows = pl.ds(pl.multiple_of(tile * TILE, 16), TILE)
@@ -302,12 +325,11 @@
         first, second = carry
         rows = pl.ds(pl.multiple_of(tile * TILE, 16), TILE)
         sums, squares = [], []
-        for chunk in chunks:
+        for chunk in narrow:
             out = by_frame(wide[rows, chunk]) * excited[:, chunk]
             out = by_frame(front[rows, chunk].astype(F32)) + out
-            out = out.reshape(TILE, CHUNK).astype(BF16)
-            work[rows, chunk] = out
-            moved = by_frame(out.astype(F32)) - pivot[:, chunk]
+            work[rows, chunk] = out.reshape(TILE, LANES).astype(BF16)
+            moved = out - pivot[:, chunk]
             sums.append(jnp.sum(moved, axis=0))
             squares.append(jnp.sum(moved * moved, axis=0))
         attn[rows, :] = dot(work[rows, :], attend[0:channels, :])
@@ -478,8 +500,8 @@
         scratch_shapes=copied
         + [
             pltpu.VMEM((stored * SEND_ROWS, LANES), F32),
-            pltpu.VMEM((groups, SEND_ROWS, LANES), BF16),
-            pltpu.VMEM((groups, SEND_ROWS, LANES), BF16),
+            pltpu.VMEM((2, groups, PART_ROWS, LANES), BF16),
+            pltpu.VMEM((2, groups, PART_ROWS, LANES), BF16),
             pltpu.VMEM((groups * SLOT_ROWS, LANES), F32),
             pltpu.VMEM((rows, WINDOW), BF16),
             pltpu.VMEM((rows, channels), BF16),
@@ -494,8 +516,8 @@
             pltpu.VMEM((stored, 2 * LANES), F32),
             pltpu.VMEM((members, stored, 2 * LANES), F32),
             dma((len(copied) + 1,)),
-            dma((groups,)),
-            dma((groups,)),
+            dma((2, groups)),
+            dma((2, groups)),
             dma((groups,)),
             dma((groups,)),
             dma((members,)),

time: 42.2 us -> 42 us (level)
  no operation moved by 1% of the time
where the time goes in v6:
time: 42 us; the launch traced here: 41.8 us
  Pallas kernels  41.2 us (98%)
  between operations  0.64 us (2%)
    pallas_call x1, Pallas kernels, shards(): pl.pallas_call(functools.partial(kernel, groups, members), out_shape=jax....  39.9 us
    pallas_call x1, Pallas kernels, shards(): pl.pallas_call(split_result, out_shape=(jax.ShapeDtypeStruct((1, stored,...  1.3 us

profile of v6, /device:TPU:0, one launch (start us, length us, event | category | flops | bytes accessed | tf_op | source)
XLA Modules:
  0.0 41.8 jit_solution(15670958118547568741)
XLA Ops:
  0.6 39.9 %shard_map.131.result_ref = f32[8,256]{1,0:T(8,128)} custom-call(f32[8,16000]{1,0:T(8,128)} %bitcast.9, s32[1,8]{1,0:T(1,128)} %dest_ref.1, bf16[400,1024]{1,0:T(8,128)(2,1)} %w0_hbm.1, bf16[1024,1024]{1,0:T(8,128)(2,1)} %expand_hbm.1, bf16[7,384,128]{2,1,0:T(8,128)(2,1)} %branch_hbm.1, bf16[1024,1024]{1,0:T(8,128)(2,1)} %merge_hbm.1, ...), custom_call_target="tpu_custom_call" | custom-call | flops 19200000000 | bytes 10000000 | tf_op jit(solution)/shard_map/pallas_call | solution.py:495
  40.5 1.3 %shard_map.132 = (f32[1,8,107]{2,1,0:T(8,128)}, f32[1,8,32]{2,1,0:T(8,128)}) custom-call(f32[8,256]{1,0:T(8,128)} %shard_map.131.result_ref), custom_call_target="tpu_custom_call" | custom-call | tf_op jit(solution)/shard_map/pallas_call | solution.py:533

commit v7 on v6

--- a/solution.py
+++ b/solution.py
@@ -250,15 +250,12 @@
 
     def rows_of_tile(side, tile):
         rows = pl.ds(pl.multiple_of(tile * TILE, 16), TILE)
-        for chunk in chunks:
-            out = jnp.maximum(dot(cols[rows, :], w0[:, chunk]), 0.0)
-            front[rows, chunk] = out.astype(BF16)
+        out = jnp.maximum(dot(cols[rows, :], w0[...]), 0.0).astype(BF16)
+        front[rows, :] = out
         start = pl.multiple_of(tile % half_tiles * TILE + side * halo, 16)
-        for chunk in chunks:
-            expanded = jnp.maximum(dot(front[rows, :], expand[:, chunk]), 0.0).astype(BF16)
-            work[rows, chunk] = expanded
-            if chunk.start == 0:
-                ping[side, pl.ds(start, TILE), :] = expanded[:, LANES : 2 * LANES]
+        expanded = jnp.maximum(dot(out, expand[...]), 0.0).astype(BF16)
+        work[rows, :] = expanded
+        ping[side, pl.ds(start, TILE), :] = expanded[:, LANES : 2 * LANES]
 
     split = FRAMES // 16
     receive(0)
@@ -303,12 +300,9 @@
 
     def merging(tile, total):
         rows = pl.ds(pl.multiple_of(tile * TILE, 16), TILE)
-        sums = []
-        for chunk in chunks:
-            merged = jnp.maximum(dot(work[rows, :], merge[:, chunk]), 0.0)
-            wide[rows, chunk] = merged
-            sums.append(jnp.sum(by_frame(merged), axis=0))
-        return total + jnp.concatenate(sums, axis=1)
+        merged = jnp.maximum(dot(work[rows, :], merge[...]), 0.0)
+        wide[rows, :] = merged
+        return total + jnp.sum(by_frame(merged), axis=0)
 
     zeros = jnp.zeros((groups, channels), F32)
     total = lax.fori_loop(0, tiles, merging, zeros)

time: 42 us -> 41.9 us (level)
  no operation moved by 1% of the time
where the time goes in v7:
time: 41.9 us; the launch traced here: 41.7 us
  Pallas kernels  41.1 us (98%)
  between operations  0.64 us (2%)
    pallas_call x1, Pallas kernels, shards(): pl.pallas_call(functools.partial(kernel, groups, members), out_shape=jax....  39.8 us
    pallas_call x1, Pallas kernels, shards(): pl.pallas_call(split_result, out_shape=(jax.ShapeDtypeStruct((1, stored,...  1.3 us

profile of v7, /device:TPU:0, one launch (start us, length us, event | category | flops | bytes accessed | tf_op | source)
XLA Modules:
  0.0 41.7 jit_solution(524910313536949685)
XLA Ops:
  0.6 39.8 %shard_map.131.result_ref = f32[8,256]{1,0:T(8,128)} custom-call(f32[8,16000]{1,0:T(8,128)} %bitcast.9, s32[1,8]{1,0:T(1,128)} %dest_ref.1, bf16[400,1024]{1,0:T(8,128)(2,1)} %w0_hbm.1, bf16[1024,1024]{1,0:T(8,128)(2,1)} %expand_hbm.1, bf16[7,384,128]{2,1,0:T(8,128)(2,1)} %branch_hbm.1, bf16[1024,1024]{1,0:T(8,128)(2,1)} %merge_hbm.1, ...), custom_call_target="tpu_custom_call" | custom-call | flops 19200000000 | bytes 10000000 | tf_op jit(solution)/shard_map/pallas_call | solution.py:489
  40.4 1.3 %shard_map.132 = (f32[1,8,107]{2,1,0:T(8,128)}, f32[1,8,32]{2,1,0:T(8,128)}) custom-call(f32[8,256]{1,0:T(8,128)} %shard_map.131.result_ref), custom_call_target="tpu_custom_call" | custom-call | tf_op jit(solution)/shard_map/pallas_call | solution.py:527
